TPU v7x, 512 devices: a whole 4x4x16 slice. The times are simulated.
512 devices in a mesh: brick: 128 (over y, z_hi, x, core), plane: 4 (over z_lo).
Axes of the slice: x: 4, y: 4, z: 16 (z_hi: 4, z_lo: 4; z = z_hi * 4 + z_lo), core: 2. Of those that a mesh axis runs over, the one named last changes fastest.
Arguments:
- positions: float32 [128, 4, 3, 4096], P('brick', 'plane'), may hold values from 0 to 64
- aux: float32 [128, 4, 4096], P('brick', 'plane'), may hold values from -1 to 1.8
- aux_prev: float32 [128, 4, 4096], P('brick', 'plane'), may hold values from -3 to 3
- resid: float32 [128, 4, 4096], P('brick', 'plane'), may hold values from -2 to 2
- types: int32 [128, 4, 4096], P('brick', 'plane'), may hold values from 0 to 7
- pair_tiles: int32 [128, 4, 1496], P('brick', 'plane'), may hold values from 0 to 63, as said below
- pair_cands: int32 [128, 4, 1496], P('brick', 'plane'), may hold values from 0 to 319, as said below
- pair_count: int32 [128, 4], P('brick', 'plane'), may hold values from 0 to 1496, as said below
- owner_tile: int32 [128, 4, 64], P('brick', 'plane'), may hold values from 0 to 255, as said below
- electroneg: float32 [8], replicated, may hold values from -3 to 3
- hardness: float32 [8], replicated, may hold values from 6 to 14
- widths: float32 [8], replicated, may hold values from 0.6 to 2
Outputs:
- charges: float32 [128, 4, 4096], P('brick', 'plane')
- next_aux: float32 [128, 4, 4096], P('brick', 'plane')
- resid_field: float32 [128, 4, 4096], P('brick', 'plane')
Inputs may be any that keep to these rules, and one draw needn't show every extreme that they name: `pair_tiles`: entries after the first pair_count[b, p] of a brick's list are not used. `pair_cands`: A used pair never names a neighbour brick beyond the ends of the brick axis. `pair_count`: at most 1496 pairs a brick, reached by some brick. `owner_tile`: for each b the values over all p and t form a permutation of 0 to 255, and each brick (b, p) has exactly 16 tiles of each value // 64.
All inputs are finite; a program needn't handle non-finite values.
Results may differ from a plain program's by a relative error of at most 0.0003.
Values sent between devices are 32-bit elements; how exact they have to be, the bound alone decides.
A program may use at most 64 MiB of HBM per device.

v0:
```python
import jax
import jax.numpy as jnp
from jax import lax
from jax.sharding import PartitionSpec as P

TX = 2
TY = 4
TILE = 64


cell_edge = 8.0
cutoff = 10.0
soften = 0.5
kappa = 1.86
pair_group = 256


def extended(block, sides, width):
    for axis, dim in sides:
        count = lax.axis_size(axis)
        forward = [(i, i + 1) for i in range(count - 1)]
        forward.append((count - 1, 0))
        backward = [(target, source) for source, target in forward]
        low = lax.ppermute(
            lax.slice_in_dim(block, block.shape[dim] - width, None, axis=dim), axis, forward
        )
        high = lax.ppermute(lax.slice_in_dim(block, 0, width, axis=dim), axis, backward)
        block = jnp.concatenate([low, block, high], axis=dim)
    return block


def lookup(type_table, type_row):
    chosen = (
        type_row[None, :] == jnp.arange(type_table.shape[0], dtype=jnp.int32)[:, None]
    ).astype(type_table.dtype)
    return jnp.sum(type_table[:, None] * chosen, axis=0)


def candidates(blocks, tile_count):
    joined = jnp.stack(blocks, axis=1)
    offsets = jnp.zeros((6, 5), jnp.float32)
    offsets = offsets.at[0, 1].set(-TX * cell_edge).at[0, 2].set(TX * cell_edge)
    offsets = offsets.at[1, 3].set(-TY * cell_edge).at[1, 4].set(TY * cell_edge)
    joined = joined + offsets[:, :, None]
    return joined.reshape(6, 5 * tile_count, TILE)


def pair_terms(home_tiles, candidate, near_ids, far_ids, in_range):
    tile_count = home_tiles.shape[1]
    near_atoms = jnp.take(home_tiles, near_ids, axis=1)
    far_atoms = jnp.take(candidate, far_ids, axis=1)
    delta_x = near_atoms[0][:, :, None] - far_atoms[0][:, None, :]
    delta_y = near_atoms[1][:, :, None] - far_atoms[1][:, None, :]
    delta_z = near_atoms[2][:, :, None] - far_atoms[2][:, None, :]
    dist_sq = delta_x * delta_x + delta_y * delta_y + delta_z * delta_z
    spacing = jnp.sqrt(dist_sq + soften * soften)
    inv_width = lax.rsqrt(near_atoms[5][:, :, None] ** 2 + far_atoms[5][:, None, :] ** 2)
    taper = jnp.square(jnp.maximum(1.0 - dist_sq / (cutoff * cutoff), 0.0))
    kernel = jax.scipy.special.erf(inv_width * spacing) / spacing * taper
    diagonal = (
        jnp.arange(TILE, dtype=jnp.int32)[:, None] == jnp.arange(TILE, dtype=jnp.int32)[None, :]
    )
    self_pairs = (far_ids == near_ids)[:, None, None] & diagonal[None]
    kept_pairs = in_range[:, None, None] & jnp.logical_not(self_pairs)
    kernel = jnp.where(kept_pairs, kernel, 0.0)
    pair_fields = jnp.einsum(
        "pij,cpj->cpi", kernel, far_atoms[3:5], precision=lax.Precision.HIGHEST
    )
    chosen = (near_ids[:, None] == jnp.arange(tile_count, dtype=jnp.int32)[None, :]).astype(
        pair_fields.dtype
    )
    return jnp.einsum("pt,cpi->cti", chosen, pair_fields, precision=lax.Precision.HIGHEST)


def sweep(home_tiles, candidate, near_list, far_list, begin_pair, end_pair, running):
    near_pad = jnp.concatenate([near_list, jnp.zeros((pair_group,), jnp.int32)])
    far_pad = jnp.concatenate([far_list, jnp.zeros((pair_group,), jnp.int32)])
    turns = (end_pair - begin_pair + pair_group - 1) // pair_group

    def advance(block_index, running):
        offset_start = begin_pair + block_index * pair_group
        near_ids = lax.dynamic_slice_in_dim(near_pad, offset_start, pair_group)
        far_ids = lax.dynamic_slice_in_dim(far_pad, offset_start, pair_group)
        in_range = offset_start + jnp.arange(pair_group, dtype=jnp.int32) < end_pair
        return running + pair_terms(home_tiles, candidate, near_ids, far_ids, in_range)

    return lax.fori_loop(0, turns, advance, running)


def on_device(
    positions,
    aux,
    aux_prev,
    resid,
    types,
    pair_tiles,
    pair_cands,
    pair_count,
    owner_tile,
    electroneg,
    hardness,
    widths,
):
    atom_count = aux.shape[-1]
    tile_count = atom_count // TILE
    type_row = types.reshape(atom_count)
    negativity = lookup(electroneg, type_row)
    hardness_row = lookup(hardness, type_row)
    radius = lookup(widths, type_row)
    charge_row = aux.reshape(atom_count)
    resid_row = resid.reshape(atom_count)
    packed = jnp.concatenate(
        [positions.reshape(3, atom_count), charge_row[None], resid_row[None], radius[None]], axis=0
    )
    rimmed = extended(packed[None, None], (("brick", 0), ("plane", 1)), 1)
    candidate = candidates(
        [rimmed[1, 1], rimmed[0, 1], rimmed[2, 1], rimmed[1, 0], rimmed[1, 2]], tile_count
    )
    home_tiles = packed.reshape(6, tile_count, TILE)
    near_list = pair_tiles.reshape(-1)
    far_list = pair_cands.reshape(-1)
    pair_total = pair_count.reshape(())
    start_total = jnp.zeros((2, tile_count, TILE), jnp.float32)
    totals = sweep(home_tiles, candidate, near_list, far_list, 0, pair_total, start_total)
    aux_field = totals[0].reshape(atom_count)
    resid_field = totals[1].reshape(atom_count)
    field = negativity + aux_field + resid_field
    global_sums = lax.psum(
        (jnp.sum(charge_row), jnp.sum(field / hardness_row), jnp.sum(1.0 / hardness_row)),
        ("brick", "plane"),
    )
    potential_level = (global_sums[0] + global_sums[1]) / global_sums[2]
    charges = (potential_level - field) / hardness_row
    stacked = jnp.stack([charge_row, charges]).reshape(2, tile_count, TILE)
    target = owner_tile.reshape(tile_count)
    planes = lax.axis_size("plane")
    gathered, gathered_slots = (
        lax.all_gather(stacked[None], "plane", axis=0, tiled=True),
        lax.all_gather(target.astype(jnp.float32)[None], "plane", axis=0, tiled=True),
    )
    whole = jnp.transpose(gathered, (1, 0, 2, 3)).reshape(2, planes * tile_count, TILE)
    slot_ids = gathered_slots.reshape(planes * tile_count).astype(jnp.int32)
    mine = lax.axis_index("plane") * tile_count + jnp.arange(tile_count, dtype=jnp.int32)
    placer = (slot_ids[None, :] == mine[:, None]).astype(jnp.float32)
    placed = jnp.einsum("sk,ckj->csj", placer, whole, precision=lax.Precision.HIGHEST)
    previous = aux_prev.reshape(tile_count, TILE)
    next_aux = 2.0 * placed[0] - previous + kappa * (placed[1] - placed[0])
    return (charges.reshape(aux.shape), next_aux.reshape(aux.shape), resid_field.reshape(aux.shape))


def solution(mesh):
    in_specs = (
        P("brick", "plane", None, None),
        P("brick", "plane", None),
        P("brick", "plane", None),
        P("brick", "plane", None),
        P("brick", "plane", None),
        P("brick", "plane", None),
        P("brick", "plane", None),
        P("brick", "plane"),
        P("brick", "plane", None),
        P(),
        P(),
        P(),
    )
    out_specs = (P("brick", "plane", None), P("brick", "plane", None), P("brick", "plane", None))
    return jax.shard_map(
        on_device, mesh=mesh, in_specs=in_specs, out_specs=out_specs, check_vma=False
    )
```

profile of v0, /device:TPU:1, one launch (start us, length us, event | category | flops | bytes accessed | tf_op | source)
XLA Modules:
  0.0 359.2 jit_solution(17657428867566629338)
XLA Ops:
  0.7 0.8 copy.57
  1.5 0.9 select_reduce_fusion.2
  2.4 0.8 fusion.37
  3.2 4.5 %collective-permute-start = (f32[1,1,6,4096]{3,2,1,0:T(8,128)S(1)}, f32[1,1,6,4096]{3,2,1,0:T(8,128)S(1)}, u32[]{:S(2)}, u32[]{:S(2)}) collective-permute-start(f32[1,1,6,4096]{3,2,1,0:T(8,128)S(1)} %fusion.37), channel_id=1, source_target_pairs={{0,4},{4,8},{8,12},{12,16},{16,20},{20,24},{24,28},{28,32},{32,36}... | collective-permute-start | bytes 294920 | tf_op jit(solution)/shard_map/ppermute | solution.py:24
  7.7 6.2 %collective-permute-start.1 = (f32[1,1,6,4096]{3,2,1,0:T(8,128)S(1)}, f32[1,1,6,4096]{3,2,1,0:T(8,128)S(1)}, u32[]{:S(2)}, u32[]{:S(2)}) collective-permute-start(f32[1,1,6,4096]{3,2,1,0:T(8,128)S(1)} %fusion.37), channel_id=1, source_target_pairs={{4,0},{8,4},{12,8},{16,12},{20,16},{24,20},{28,24},{32,28},{36,32}... | collective-permute-start | bytes 294920 | tf_op jit(solution)/shard_map/ppermute | solution.py:27
  14.0 0.8 bitcast_dynamic-update-slice_fusion.2
  15.5 0.5 broadcast.209
  16.0 2.1 fusion.46
  18.1 1.4 reduce.31
  19.5 0.9 reduce.17
  20.5 0.6 divide_reduce_fusion
  21.3 0.6 fusion.48
  21.9 0.6 fusion.47
  22.5 1.3 and_reduce_fusion
  23.9 1.4 scatter.14
  25.3 1.9 dynamic-slice.29
  28.4 1.4 scatter.15
  30.9 5.8 %all-gather = f32[4,1,64]{2,1,0:T(1,128)S(1)} all-gather(f32[1,1,64]{2,1,0:T(1,128)S(1)} %convert_element_type.28), channel_id=2, replica_groups=mesh['brick'=128,'plane'=4] {'plane'}, dimensions={0}, use_global_device_ids=true | all-gather | bytes 1280 | tf_op jit(solution)/shard_map/all_gather | solution.py:139
  36.8 3.3 collective-permute-start.2
  40.1 3.8 %collective-permute-start.3 = (f32[3,1,6,4096]{3,2,1,0:T(8,128)S(1)}, f32[3,1,6,4096]{3,2,1,0:T(8,128)S(1)}, u32[]{:S(2)}, u32[]{:S(2)}) collective-permute-start(f32[3,1,6,4096]{3,2,1,0:T(8,128)S(1)} %pad_maximum_fusion), channel_id=1, source_target_pairs={{1,0},{2,1},{3,2},{0,3},{5,4},{6,5},{7,6},{4,7},{9,8},{10,9},{11,1... | collective-permute-start | bytes 884744 | tf_op jit(solution)/shard_map/ppermute | solution.py:27
  43.9 3.3 collective-permute-done.2
  47.3 4.1 %collective-permute-done.3 = f32[3,1,6,4096]{3,2,1,0:T(8,128)S(1)} collective-permute-done((f32[3,1,6,4096]{3,2,1,0:T(8,128)S(1)}, f32[3,1,6,4096]{3,2,1,0:T(8,128)S(1)}, u32[]{:S(2)}, u32[]{:S(2)}) %collective-permute-start.3) | collective-permute-done | bytes 294944 | tf_op jit(solution)/shard_map/ppermute | solution.py:27
  51.7 0.4 stack.12
  52.4 0.6 copy.46
  53.0 57.3 %while.14 = (s32[]{:T(128)}, f32[2,64,64]{1,2,0:T(8,128)S(1)}, s32[]{:T(128)}, s32[1752]{0:T(1024)S(1)}, f32[6,320,64]{2,0,1:T(8,128)S(1)}, /*index=5*/s32[]{:T(...) while((s32[]{:T(128)}, f32[2,64,64]{1,2,0:T(8,128)S(1)}, ...), condition=%wide.region_6.0_spmd, body=%wide.region_5.0_spmd.sunk | while | flops 72616448 | bytes 5868207 | solution.py:87
  53.0 0.7 dynamic-slice_compare_fusion.2
  53.8 1.0 gather_fusion.1
  54.8 0.3 select_bitcast_fusion.5
  55.2 0.4 slice_multiply_fusion.6
  55.6 1.0 gather_fusion
  56.6 0.3 select_bitcast_fusion.4
  56.9 0.4 slice_multiply_fusion.5
  57.4 23.9 %fusion.66 = f32[2,256,64]{2,0,1:T(2,128)S(1)} fusion(f32[256,64]{1,0:T(8,128)S(1)} %bitcast.106, f32[256,64]{1,0:T(8,128)S(1)} %bitcast.102, f32[256,64]{1,0:T(8,128)S(1)} %bitcast.107, f32[256,64]{1,0:T(8,128)S(1)} %bitcast.103, f32[256,64]{1,0:T(8,128)S(1)} %bitcast.108, f32[256,64]{1,0:T(8,128)S(1)} %bitcast.104, f32[256,64]{1,0:T(8,128)S(1)} %bitcast.105, ...), kind=kOutput, calls=%fused_computation.24.clone.3 | convolution fusion | flops 47185920 | bytes 1451008 | tf_op jit(solution)/shard_map/while/body/pij,cpj->cpi/dot_general | solution.py:66
  81.3 0.4 fusion.67
  81.7 0.7 dynamic-slice_compare_fusion.2
  82.4 1.0 gather_fusion.1
  83.5 0.3 select_bitcast_fusion.5
  83.8 0.4 slice_multiply_fusion.6
  84.2 1.0 gather_fusion
  85.3 0.3 select_bitcast_fusion.4
  85.6 0.4 slice_multiply_fusion.5
  86.0 23.9 %fusion.66 = f32[2,256,64]{2,0,1:T(2,128)S(1)} fusion(f32[256,64]{1,0:T(8,128)S(1)} %bitcast.106, f32[256,64]{1,0:T(8,128)S(1)} %bitcast.102, f32[256,64]{1,0:T(8,128)S(1)} %bitcast.107, f32[256,64]{1,0:T(8,128)S(1)} %bitcast.103, f32[256,64]{1,0:T(8,128)S(1)} %bitcast.108, f32[256,64]{1,0:T(8,128)S(1)} %bitcast.104, f32[256,64]{1,0:T(8,128)S(1)} %bitcast.105, ...), kind=kOutput, calls=%fused_computation.24.clone.3 | convolution fusion | flops 47185920 | bytes 1451008 | tf_op jit(solution)/shard_map/while/body/pij,cpj->cpi/dot_general | solution.py:66
  109.9 0.4 fusion.67
  110.4 0.6 fusion.44
  112.5 230.6 %all-reduce.2 = (f32[]{:T(128)}, f32[]{:T(128)}) all-reduce(f32[]{:T(128)S(6)} %add.163, f32[]{:T(128)} %divide_reduce_fusion), channel_id=1, replica_groups=mesh['brick'=128,'plane'=4] {'brick','plane'}, use_global_device_ids=true, to_apply=%region_1.0 | all-reduce | flops 2 | bytes 16 | tf_op jit(solution)/shard_map/psum | solution.py:128
  344.5 12.2 %all_gather.6 = f32[4,2,64,64]{3,2,1,0:T(8,128)S(1)} all-gather(f32[1,2,64,64]{3,2,1,0:T(8,128)S(1)} %pad_maximum_fusion.3), channel_id=1, replica_groups=mesh['brick'=128,'plane'=4] {'plane'}, dimensions={0}, use_global_device_ids=true | all-gather | bytes 163840 | tf_op jit(solution)/shard_map/all_gather | solution.py:138
  358.0 0.6 subtract_add_fusion
  358.6 0.6 subtract_divide_fusion
  (71 shorter events, 3.5 us)
Async XLA Ops:
  0.6 30.1 %copy-start = (f32[1,1,4096]{2,1,0:T(1,128)S(1)}, f32[1,1,4096]{2,1,0:T(1,128)}, u32[]{:S(2)}) copy-start(f32[1,1,4096]{2,1,0:T(1,128)} %param.23) | copy-start | bytes 49156
  0.6 30.0 %copy-start.3 = (s32[1,1,1496]{2,1,0:T(1,128)S(1)}, s32[1,1,1496]{2,1,0:T(1,128)}, u32[]{:S(2)}) copy-start(s32[1,1,1496]{2,1,0:T(1,128)} %param.28) | copy-start | bytes 17956
  0.7 30.1 %copy-start.4 = (s32[1,1,1496]{2,1,0:T(1,128)S(1)}, s32[1,1,1496]{2,1,0:T(1,128)}, u32[]{:S(2)}) copy-start(s32[1,1,1496]{2,1,0:T(1,128)} %param.27) | copy-start | bytes 17956
  0.7 30.2 %copy-start.5 = (s32[1,1,64]{2,1,0:T(1,128)S(1)}, s32[1,1,64]{2,1,0:T(1,128)}, u32[]{:S(2)}) copy-start(s32[1,1,64]{2,1,0:T(1,128)} %param.30) | copy-start | bytes 772
  3.2 33.5 %collective-permute-start = (f32[1,1,6,4096]{3,2,1,0:T(8,128)S(1)}, f32[1,1,6,4096]{3,2,1,0:T(8,128)S(1)}, u32[]{:S(2)}, u32[]{:S(2)}) collective-permute-start(f32[1,1,6,4096]{3,2,1,0:T(8,128)S(1)} %fusion.37), channel_id=1, source_target_pairs={{0,4},{4,8},{8,12},{12,16},{16,20},{20,24},{24,28},{28,32},{32,36}... | collective-permute-start | bytes 294920 | tf_op jit(solution)/shard_map/ppermute | solution.py:24
  7.7 29.0 %collective-permute-start.1 = (f32[1,1,6,4096]{3,2,1,0:T(8,128)S(1)}, f32[1,1,6,4096]{3,2,1,0:T(8,128)S(1)}, u32[]{:S(2)}, u32[]{:S(2)}) collective-permute-start(f32[1,1,6,4096]{3,2,1,0:T(8,128)S(1)} %fusion.37), channel_id=1, source_target_pairs={{4,0},{8,4},{12,8},{16,12},{20,16},{24,20},{28,24},{32,28},{36,32}... | collective-permute-start | bytes 294920 | tf_op jit(solution)/shard_map/ppermute | solution.py:27
  36.8 10.5 %collective-permute-start.2 = (f32[3,1,6,4096]{3,2,1,0:T(8,128)S(1)}, f32[3,1,6,4096]{3,2,1,0:T(8,128)S(1)}, u32[]{:S(2)}, u32[]{:S(2)}) collective-permute-start(f32[3,1,6,4096]{3,2,1,0:T(8,128)S(1)} %pad_maximum_fusion), channel_id=1, source_target_pairs={{0,1},{1,2},{2,3},{3,0},{4,5},{5,6},{6,7},{7,4},{8,9},{9,10},{10,1... | collective-permute-start | bytes 884744 | tf_op jit(solution)/shard_map/ppermute | solution.py:24
  40.1 11.3 %collective-permute-start.3 = (f32[3,1,6,4096]{3,2,1,0:T(8,128)S(1)}, f32[3,1,6,4096]{3,2,1,0:T(8,128)S(1)}, u32[]{:S(2)}, u32[]{:S(2)}) collective-permute-start(f32[3,1,6,4096]{3,2,1,0:T(8,128)S(1)} %pad_maximum_fusion), channel_id=1, source_target_pairs={{1,0},{2,1},{3,2},{0,3},{5,4},{6,5},{7,6},{4,7},{9,8},{10,9},{11,1... | collective-permute-start | bytes 884744 | tf_op jit(solution)/shard_map/ppermute | solution.py:27
  110.3 247.6 %copy-start.2 = (f32[1,1,4096]{2,1,0:T(1,128)S(1)}, f32[1,1,4096]{2,1,0:T(1,128)}, u32[]{:S(2)}) copy-start(f32[1,1,4096]{2,1,0:T(1,128)} %param.24) | copy-start | bytes 49156
  357.9 1.3 copy-start.1
where the time goes:
time: 362 us; the launch traced here: 359 us
  blocking collectives  249 us (69%)
  matrix products  48.9 us (14%)
  starting transfers between devices  17.8 us (5%)
  other arithmetic  15.6 us (4%)
  local copies, waits for them, and re-layouts  15 us (4%)
  waiting for transfers between devices  7.42 us (2%)
  between operations  5.63 us (2%)
    psum x1, blocking collectives, on_device(): lax.psum((jnp.sum(charge_row), jnp.sum(field / hardness_row), jnp.sum(1.0...  231 us
    dot_general x2, matrix products, pair_terms(): jnp.einsum('pij,cpj->cpi', kernel, far_atoms[3:5], precision=lax.Precisio...  47.9 us
    all_gather x1, blocking collectives, on_device(): lax.all_gather(stacked[None], 'plane', axis=0, tiled=True)  12.2 us
    ppermute x2, starting transfers between devices, extended(): lax.ppermute(lax.slice_in_dim(block, 0, width, axis=dim), axis, backward)  9.97 us
    ppermute x2, starting transfers between devices, extended(): lax.ppermute(lax.slice_in_dim(block, block.shape[dim] - width, None, axis...  7.81 us
  transfers between devices with their start and end apart: 4, of which 2 were waited for; matrix products, arithmetic and copies ran while one was open for 4% of the time, Pallas kernels for 0%

commit v1 on v0

v1 whole, which is shorter than its diff:
```python
import functools

import jax
import jax.numpy as jnp
from jax import lax
from jax.experimental import pallas as pl
from jax.experimental.pallas import tpu as pltpu
from jax.sharding import PartitionSpec as P

F32 = jnp.float32
BF = jnp.bfloat16
HI = lax.Precision.HIGHEST
MESH = pl.DeviceIdType.MESH
kappa = 1.86

PB = 12
SB = 13
NT = 320


def sort_kernel(tiles, cands, count, codes, total, selfs, tr, cr):
    n = tiles.shape[1]
    one = lax.broadcasted_iota(jnp.int32, (1, 128), 1)
    tr[...] = jnp.full((128, 128), 64.0, F32)
    cr[...] = jnp.zeros((16, 128), F32)
    for j in range(PB):
        w = min(128, n - 128 * j)
        tr[j : j + 1, :w] = tiles[:, 128 * j : 128 * j + w].astype(F32)
        cr[j : j + 1, :w] = cands[:, 128 * j : 128 * j + w].astype(F32)
    prow = lax.broadcasted_iota(jnp.int32, (16, 128), 0) * 128 + lax.broadcasted_iota(jnp.int32, (16, 128), 1)
    used = prow < count[0, 0]
    t = jnp.where(used, tr[:16], 64.0)
    c = jnp.where(used, cr[...], 0.0)
    tr[:16] = t
    tcol = tr[...].T
    lane = lax.broadcasted_iota(jnp.int32, (128, 128), 1)
    rowi = lax.broadcasted_iota(jnp.int32, (128, 128), 0)
    lanef = lane.astype(F32)
    before = jnp.where(lane < rowi, 1.0, 0.0).astype(BF)
    hot = [tcol[:, j : j + 1] == lanef for j in range(PB)]
    hotf = [jnp.where(h, 1.0, 0.0) for h in hot]
    sums = [jnp.sum(h, axis=0, keepdims=True) for h in hotf]
    counts = sum(sums)
    counts = jnp.where(one < 64, counts, 0.0)
    half = jnp.floor((counts + 1.0) * 0.5)
    starts = 2.0 * jnp.dot(jnp.broadcast_to(half, (8, 128)), jnp.where(rowi < lane, 1.0, 0.0), precision=HI, preferred_element_type=F32)[:1]
    starts = jnp.where(one < 64, starts, 8192.0)
    total[...] = jnp.broadcast_to(jnp.sum(half, axis=1, keepdims=True), (8, 128)).astype(jnp.int32)
    out = jnp.zeros((8, SB * 128), F32)
    slot = lax.broadcasted_iota(jnp.int32, (128, SB * 128), 1).astype(F32)
    selfrow = jnp.zeros((1, 128), F32)
    e = float(NT) - c
    e = jnp.where(used, e, 0.0)
    ehi = jnp.floor(e * 0.5)
    elo = e - 2.0 * ehi
    same = jnp.where(t == c, 1.0, 0.0)
    r8 = lax.broadcasted_iota(jnp.int32, (8, 128), 0)
    for j in range(PB):
        rank = jnp.dot(before, hotf[j].astype(BF), preferred_element_type=F32)
        pos = jnp.sum(jnp.where(hot[j], rank + starts, 0.0), axis=1, keepdims=True)
        starts = starts + sums[j]
        vals = jnp.where(r8 == 0, ehi[j : j + 1], jnp.where(r8 == 1, elo[j : j + 1], jnp.where(r8 == 2, t[j : j + 1], same[j : j + 1])))
        put = jnp.where(pos == slot, 1.0, 0.0).astype(BF)
        out = out + jnp.dot(vals.astype(BF), put, preferred_element_type=F32)
        selfrow = selfrow + jnp.dot(vals.astype(BF), hotf[j].astype(BF), preferred_element_type=F32)[3:4]
    code = out[2:3] * 512.0 + (float(NT) - (2.0 * out[0:1] + out[1:2]))
    codes[...] = code.astype(jnp.int32)
    selfs[...] = jnp.broadcast_to(selfrow, (8, 128))


def sort_call(tiles, cands, count):
    vm = pl.BlockSpec(memory_space=pltpu.VMEM)
    return pl.pallas_call(
        sort_kernel,
        out_shape=[jax.ShapeDtypeStruct((1, SB * 128), jnp.int32), jax.ShapeDtypeStruct((8, 128), jnp.int32), jax.ShapeDtypeStruct((8, 128), F32)],
        in_specs=[vm, vm, pl.BlockSpec(memory_space=pltpu.SMEM)],
        out_specs=[vm, vm, vm],
        scratch_shapes=[pltpu.VMEM((128, 128), F32), pltpu.VMEM((16, 128), F32)],
        name="pairs_sort",
    )(tiles, cands, count)

NR = 160
UN = 8


def pair_kernel(codes, total, widths, chi, hard, selfs, own, halo, fe, rf, G, C, HB, CH, acc, FR):
    lane = lax.broadcasted_iota(jnp.int32, (8, 128), 1)
    row = lax.broadcasted_iota(jnp.int32, (8, 128), 0)
    low = lane < 64
    for b in range(5):
        at = [own[c] if b == 0 else halo[b - 1, c] for c in range(6)]
        if b in (1, 2):
            at[0] = at[0] + (-16.0 if b == 1 else 16.0)
        if b in (3, 4):
            at[1] = at[1] + (-32.0 if b == 3 else 32.0)
        s = jnp.zeros((32, 128), F32)
        for t in range(8):
            s = jnp.where(at[5] == float(t), widths[t], s)
        for c, x in enumerate((at[0] * 0.1, at[1] * 0.1, at[2] * 0.1, at[3] * 0.1, at[4] * 0.1, s * s * 0.01)):
            G[pl.ds(c * NR + b * 32, 32), :] = x
    G[pl.ds(6 * NR, 2 * NR), :] = jnp.zeros((2 * NR, 128), F32)

    def halves(x):
        y = pltpu.roll(x, 64, 1)
        return jnp.where(low, x, y), jnp.where(low, y, x)

    def prep(g, carry):
        c0, c1 = halves(G[pl.ds(g, 8, stride=NR), :])
        C[g * 2] = c0
        C[g * 2 + 1] = c1
        return carry

    lax.fori_loop(0, NR, prep, 0, unroll=8)
    C[NT] = jnp.where((row == 3) | (row == 4), 0.0, C[0])

    def prep_home(r, carry):
        v = G[pl.ds(r, 8, stride=NR), :]
        x = v[:, 0:1]
        y = v[:, 64:65]
        cen = jnp.where(low, jnp.broadcast_to(x, (8, 128)), jnp.broadcast_to(y, (8, 128)))
        cen = jnp.where(row < 3, cen, 0.0)
        a = v - cen
        n = jnp.sum(jnp.where(row < 3, a * a, 0.0), axis=0, keepdims=True) + 0.0025
        f = jnp.where(row < 3, -2.0 * a, jnp.where(row == 3, n, jnp.where(row == 5, a, 0.0)))
        c0, c1 = halves(cen)
        CH[r * 2] = c0
        CH[r * 2 + 1] = c1
        FR[pl.ds(pl.multiple_of(r * 8, 8), 8), :] = f
        return carry

    lax.fori_loop(0, 32, prep_home, 0, unroll=4)
    for g in range(2):
        t = FR[pl.ds(128 * g, 128), :].T
        for r in range(16):
            for k, col in enumerate((0, 1, 2, 3, 5)):
                w = jnp.broadcast_to(t[:, 8 * r + col : 8 * r + col + 1], (128, 128))
                HB[k, 32 * g + 2 * r] = w[:64]
                HB[k, 32 * g + 2 * r + 1] = w[64:]
    acc[...] = jnp.zeros_like(acc)

    def step(i, carry):
        for u in range(UN):
            k1 = codes[0, 2 * UN * i + 2 * u]
            k2 = codes[0, 2 * UN * i + 2 * u + 1]
            h = lax.shift_right_logical(k1, 9)
            v = jnp.where(low, C[k1 & 511], C[k2 & 511]) - CH[h]
            n = jnp.sum(jnp.where(row < 3, v * v, 0.0), axis=0, keepdims=True)
            xs = [jnp.broadcast_to(v[k : k + 1], (8, 128)) for k in range(6)]
            n = jnp.broadcast_to(n, (8, 128))
            for q in range(8):
                rows = pl.ds(8 * q, 8)
                d = (HB[3, h, rows] + n) + HB[0, h, rows] * xs[0] + HB[1, h, rows] * xs[1] + HB[2, h, rows] * xs[2]
                w = lax.rsqrt(HB[4, h, rows] + xs[5])
                r = lax.rsqrt(d)
                e = lax.erf(d * r * w)
                m = jnp.maximum(1.0025 - d, 0.0)
                kk = (e * r) * (m * m)
                acc[0, h, rows] = acc[0, h, rows] + kk * xs[3]
                acc[1, h, rows] = acc[1, h, rows] + kk * xs[4]
        return carry

    lax.fori_loop(0, lax.div(total[0, 0] + UN - 1, UN), step, 0)
    def finish(r, carry):
        for f, ref in enumerate((fe, rf)):
            ref[pl.ds(r, 1), :] = jnp.sum(acc[f, pl.ds(2 * r, 2)].reshape(128, 128).T, axis=0, keepdims=True)
        return carry

    lax.fori_loop(0, 32, finish, 0, unroll=4)
    lane32 = lax.broadcasted_iota(jnp.int32, (32, 128), 1)
    row32 = lax.broadcasted_iota(jnp.int32, (32, 128), 0)
    n = jnp.broadcast_to(selfs[0:1], (32, 128))
    even = jnp.sum(jnp.where(lane32 == 2 * row32, n, 0.0), axis=1, keepdims=True)
    odd = jnp.sum(jnp.where(lane32 == 2 * row32 + 1, n, 0.0), axis=1, keepdims=True)
    times = jnp.where(lane32 < 64, even, odd)
    s2 = jnp.zeros((32, 128), F32)
    ch = jnp.zeros((32, 128), F32)
    eta = jnp.zeros((32, 128), F32)
    for t in range(8):
        hit = own[5] == float(t)
        s2 = jnp.where(hit, widths[t] * widths[t], s2)
        ch = jnp.where(hit, chi[t], ch)
        eta = jnp.where(hit, hard[t], eta)
    itself = times * (2.0 * lax.erf(0.5 * lax.rsqrt(s2 + s2)))
    residual = rf[...] - itself * own[4]
    field = ch + (fe[...] - itself * own[3]) + residual
    rf[...] = residual
    fe[...] = field / eta


def pair_call(codes, total, widths, chi, hard, selfs, own, halo):
    sm = pl.BlockSpec(memory_space=pltpu.SMEM)
    vm = pl.BlockSpec(memory_space=pltpu.VMEM)
    return pl.pallas_call(
        pair_kernel,
        out_shape=[jax.ShapeDtypeStruct((32, 128), F32)] * 2,
        in_specs=[sm] * 5 + [vm] * 3,
        out_specs=[vm, vm],
        scratch_shapes=[
            pltpu.VMEM((8 * NR, 128), F32),
            pltpu.VMEM((NT + 1, 8, 128), F32),
            pltpu.VMEM((5, 64, 64, 128), F32),
            pltpu.VMEM((64, 8, 128), F32),
            pltpu.VMEM((2, 64, 64, 128), F32),
            pltpu.VMEM((256, 128), F32),
        ],
        compiler_params=pltpu.CompilerParams(vmem_limit_bytes=40 * 2**20),
        name="pairs",
    )(codes, total, widths, chi, hard, selfs, own, halo)


def exchange_kernel(pos, aux, resid, types, owner, hard, own, halo, early, send, recv):
    nb, npl = lax.axis_size("brick"), lax.axis_size("plane")
    b, p = lax.axis_index("brick"), lax.axis_index("plane")
    below, above = lax.rem(b + nb - 1, nb), lax.rem(b + 1, nb)
    barrier = pltpu.get_barrier_semaphore()
    mates = [lax.rem(p + k, npl) for k in range(1, npl)]
    for d in [(below, p), (above, p)] + [(b, q) for q in mates]:
        pl.semaphore_signal(barrier, inc=1, device_id=d, device_id_type=MESH)
    for r in range(32):
        at = pl.ds(128 * r, 128)
        for c in range(3):
            own[c, r : r + 1, :] = pos[c : c + 1, at]
        own[3, r : r + 1, :] = aux[:, at]
        own[4, r : r + 1, :] = resid[:, at]
        own[5, r : r + 1, :] = types[:, at].astype(F32)
    inverse = jnp.zeros((32, 128), F32)
    ty = own[5]
    for t in range(8):
        inverse = jnp.where(ty == float(t), 1.0 / jnp.full((32, 128), hard[t], F32), inverse)
    early[p, 0] = own[3]
    early[p, 1] = inverse
    src = lax.broadcasted_iota(jnp.int32, (64, 128), 0)
    lane = lax.broadcasted_iota(jnp.int32, (64, 128), 1) - 32 * p
    inside = (lane >= 0) & (lane < 32)
    ids = jnp.broadcast_to(owner[...].astype(F32), (8, 64))
    evens = jnp.dot(ids, jnp.where(inside & (src == 2 * lane), 1.0, 0.0), precision=HI, preferred_element_type=F32)
    odds = jnp.dot(ids, jnp.where(inside & (src == 2 * lane + 1), 1.0, 0.0), precision=HI, preferred_element_type=F32)
    early[p, 2, 0:8, :] = evens
    early[p, 2, 8:16, :] = odds
    early[p, 2, 16:32, :] = jnp.zeros((16, 128), F32)
    pl.semaphore_wait(barrier, 1 + npl)

    def copy(s, d, k, to):
        return pltpu.make_async_remote_copy(
            src_ref=s, dst_ref=d, send_sem=send.at[k], recv_sem=recv.at[k], device_id=to, device_id_type=MESH
        )

    left, right = lax.rem(p + npl - 1, npl), lax.rem(p + 1, npl)
    copies = [
        copy(own, halo.at[2], 2, (b, right)),
        copy(own, halo.at[3], 3, (b, left)),
        copy(own, halo.at[0], 0, (above, p)),
        copy(own, halo.at[1], 1, (below, p)),
    ] + [copy(early.at[p], early.at[p], 4 + k, (b, q)) for k, q in enumerate(mates)]
    for c in copies:
        c.start()
    for c in copies:
        c.wait()


def exchange(pos, aux, resid, types, owner, hard):
    vm = pl.BlockSpec(memory_space=pltpu.VMEM)
    return pl.pallas_call(
        exchange_kernel,
        out_shape=[
            jax.ShapeDtypeStruct((6, 32, 128), F32),
            jax.ShapeDtypeStruct((4, 6, 32, 128), F32),
            jax.ShapeDtypeStruct((4, 3, 32, 128), F32),
        ],
        in_specs=[vm] * 5 + [pl.BlockSpec(memory_space=pltpu.SMEM)],
        out_specs=[vm] * 3,
        scratch_shapes=[pltpu.SemaphoreType.DMA((7,)), pltpu.SemaphoreType.DMA((7,))],
        compiler_params=pltpu.CompilerParams(collective_id=0, has_side_effects=True),
        name="exchange",
    )(pos, aux, resid, types, owner, hard)


LOW = 8


def level_kernel(fe, early, prev, charges, nxt, got, near, far, s1, r1, s2, r2, s3, r3):
    nb, npl = lax.axis_size("brick"), lax.axis_size("plane")
    high = nb // LOW
    b, p = lax.axis_index("brick"), lax.axis_index("plane")
    bl, bh = lax.rem(b, LOW), lax.div(b, LOW)
    mates = [lax.rem(p + k, npl) for k in range(1, npl)]
    lows = [lax.rem(bl + k, LOW) for k in range(1, LOW)]
    highs = [lax.rem(bh + k, high) for k in range(1, high)]
    barrier = pltpu.get_barrier_semaphore()
    for q in mates:
        pl.semaphore_signal(barrier, inc=1, device_id=(b, q), device_id_type=MESH)
    for q in lows:
        pl.semaphore_signal(barrier, inc=1, device_id=(bh * LOW + q, p), device_id_type=MESH)
    for q in highs:
        pl.semaphore_signal(barrier, inc=1, device_id=(q * LOW + bl, p), device_id_type=MESH)
    got[p] = fe[...]
    pl.semaphore_wait(barrier, npl - 1 + LOW - 1 + high - 1)

    def copy(s, d, ss, rs, to):
        return pltpu.make_async_remote_copy(
            src_ref=s, dst_ref=d, send_sem=ss, recv_sem=rs, device_id=to, device_id_type=MESH
        )

    first = [copy(got.at[p], got.at[p], s1.at[k], r1.at[k], (b, q)) for k, q in enumerate(mates)]
    for c in first:
        c.start()
    evens = sum(early[q, 2, 0:1, :] for q in range(4))
    odds = sum(early[q, 2, 8:9, :] for q in range(4))
    slot = (64 * p + 2 * lax.broadcasted_iota(jnp.int32, (32, 128), 0)).astype(F32)
    place = jnp.concatenate(
        [
            jnp.where(evens == slot, 1.0, 0.0),
            jnp.where(odds == slot + 1.0, 1.0, 0.0),
            jnp.where(evens == slot + 1.0, 1.0, 0.0),
            jnp.where(odds == slot, 1.0, 0.0),
        ],
        axis=0,
    )
    low = lax.broadcasted_iota(jnp.int32, (32, 128), 1) < 64

    def placed(x):
        y = jnp.dot(place, x, precision=HI, preferred_element_type=F32)
        return jnp.where(low, y[0:32], y[32:64]) + pltpu.roll(jnp.where(low, y[64:96], y[96:128]), 64, 1)

    aux = placed(early[:, 0].reshape(128, 128))
    inverse = placed(early[:, 1].reshape(128, 128))

    def fold(x):
        s = x[0:8]
        for k in range(1, 16):
            s = s + x[8 * k : 8 * k + 8]
        return s[0:4] + s[4:8]

    sum_aux = fold(early[:, 0].reshape(128, 128))
    sum_inv = fold(early[:, 1].reshape(128, 128))
    for c in first:
        c.wait()
    fes = got[...].reshape(128, 128)
    near[bl] = jnp.concatenate([sum_aux + fold(fes), sum_inv], axis=0)
    second = [copy(near.at[bl], near.at[bl], s2.at[k], r2.at[k], (bh * LOW + q, p)) for k, q in enumerate(lows)]
    for c in second:
        c.start()
    moved = placed(fes)
    for c in second:
        c.wait()
    total = near[0]
    for k in range(1, LOW):
        total = total + near[k]
    far[bh] = total
    third = [copy(far.at[bh], far.at[bh], s3.at[k], r3.at[k], (q * LOW + bl, p)) for k, q in enumerate(highs)]
    for c in third:
        c.start()
    for c in third:
        c.wait()
    total = far[0]
    for k in range(1, 16):
        total = total + far[k]
    top = jnp.sum(jnp.sum(total[0:4], axis=1, keepdims=True), axis=0, keepdims=True)
    bottom = jnp.sum(jnp.sum(total[4:8], axis=1, keepdims=True), axis=0, keepdims=True)
    level = jnp.broadcast_to(top / bottom, (32, 128))
    charges[...] = level * early[p, 1] - fe[...]
    nxt[...] = 2.0 * aux - prev[...] + kappa * (level * inverse - moved - aux)


def finish(fe, early, prev):
    vm = pl.BlockSpec(memory_space=pltpu.VMEM)
    dma = pltpu.SemaphoreType.DMA
    return pl.pallas_call(
        level_kernel,
        out_shape=[jax.ShapeDtypeStruct((32, 128), F32)] * 2,
        in_specs=[vm] * 3,
        out_specs=[vm] * 2,
        scratch_shapes=[
            pltpu.VMEM((4, 32, 128), F32),
            pltpu.VMEM((LOW, 8, 128), F32),
            pltpu.VMEM((16, 8, 128), F32),
            dma((3,)), dma((3,)), dma((7,)), dma((7,)), dma((15,)), dma((15,)),
        ],
        compiler_params=pltpu.CompilerParams(collective_id=1, has_side_effects=True),
        name="level",
    )(fe, early, prev)


def on_device(positions, aux, aux_prev, resid, types, pair_tiles, pair_cands, pair_count, owner_tile, electroneg, hardness, widths):
    own, halo, early = exchange(
        positions.reshape(3, -1), aux.reshape(1, -1), resid.reshape(1, -1), types.reshape(1, -1), owner_tile.reshape(1, -1), hardness
    )
    codes, total, selfs = sort_call(pair_tiles.reshape(1, -1), pair_cands.reshape(1, -1), pair_count)
    fe, rf = pair_call(codes, total, widths, electroneg, hardness, selfs, own, halo)
    charges, nxt = finish(fe, early, aux_prev.reshape(32, 128))
    return charges.reshape(aux.shape), nxt.reshape(aux.shape), rf.reshape(aux.shape)


def solution(mesh):
    s4, s3, s2 = P("brick", "plane", None, None), P("brick", "plane", None), P("brick", "plane")
    return jax.shard_map(
        on_device,
        mesh=mesh,
        in_specs=(s4, s3, s3, s3, s3, s3, s3, s2, s3, P(), P(), P()),
        out_specs=(s3, s3, s3),
        check_vma=False,
    )
```

time: 362 us -> 96.8 us (0.27)
  blocking collectives: 249 us -> 0 us
  Pallas kernels: 0 us -> 86.9 us
  matrix products: 48.9 us -> 0 us
  starting transfers between devices: 17.8 us -> 0 us
  other arithmetic: 15.6 us -> 0 us
  waiting for transfers between devices: 7.42 us -> 0 us
  local copies, waits for them, and re-layouts: 15 us -> 7.96 us
  between operations: 5.63 us -> 1.32 us
    psum x1 -> x0, blocking collectives: 231 us -> none  [on_device(): lax.psum((jnp.sum(charge_row), jnp.sum(field / hardness_row), jnp.sum(1.0...]
    pallas_call x0 -> x4, Pallas kernels: none -> 86.9 us  [the longest x1 46.8 us: finish(): pl.pallas_call(level_kernel, out_shape=[jax.ShapeDtypeStruct((32, 128), F...]
    dot_general x5 -> x0, matrix products: 48.9 us -> none  [the longest x2 47.9 us: pair_terms(): jnp.einsum('pij,cpj->cpi', kernel, far_atoms[3:5], precision=lax.Precisio...]
    all_gather x2 -> x0, blocking collectives: 18 us -> none  [the longest x1 12.2 us: on_device(): lax.all_gather(stacked[None], 'plane', axis=0, tiled=True)]
    ppermute x4 -> x0, starting transfers between devices: 17.8 us -> none  [the longest x2 9.97 us: extended(): lax.ppermute(lax.slice_in_dim(block, 0, width, axis=dim), axis, backward)]
    ppermute x4 -> x0, waiting for transfers between devices: 7.42 us -> none  [the longest x2 4.07 us: extended(): lax.ppermute(lax.slice_in_dim(block, 0, width, axis=dim), axis, backward)]
    unnamed x17 -> x23, local copies, waits for them, and re-layouts: 1.42 us -> 7.96 us
    reduce_sum x4 -> x0, other arithmetic: 4.21 us -> none  [the longest x1 2.09 us: on_device(): jnp.sum(charge_row)]
  transfers between devices with their start and end apart: 4 -> 0, of which waited for: 2 -> 0; matrix products, arithmetic and copies ran while one was open for 4% -> 0% of each run, Pallas kernels for 0% -> 0%
where the time goes in v1:
time: 96.8 us; the launch traced here: 96.2 us
  Pallas kernels  86.9 us (90%)
  local copies, waits for them, and re-layouts  7.96 us (8%)
  between operations  1.32 us (1%)
    pallas_call x1, Pallas kernels, finish(): pl.pallas_call(level_kernel, out_shape=[jax.ShapeDtypeStruct((32, 128), F...  46.8 us
    pallas_call x1, Pallas kernels, exchange(): pl.pallas_call(exchange_kernel, out_shape=[jax.ShapeDtypeStruct((6, 32, 1...  19.8 us
    pallas_call x1, Pallas kernels, pair_call(): pl.pallas_call(pair_kernel, out_shape=[jax.ShapeDtypeStruct((32, 128), F3...  15.2 us
    unnamed x23, local copies, waits for them, and re-layouts  7.96 us
    pallas_call x1, Pallas kernels, sort_call(): pl.pallas_call(sort_kernel, out_shape=[jax.ShapeDtypeStruct((1, SB * 128)...  5.1 us

profile of v1, /device:TPU:1, one launch (start us, length us, event | category | flops | bytes accessed | tf_op | source)
XLA Modules:
  0.0 96.2 jit_solution(1493695770551240695)
XLA Ops:
  0.6 1.5 %copy.17 = f32[1,1,3,4096]{3,2,1,0:T(4,128)} copy(f32[1,1,3,4096]{3,1,2,0:T(1,128)} %param.12) | data formatting | bytes 98304
  2.1 19.8 %exchange.1 = (f32[6,32,128]{2,1,0:T(8,128)}, f32[4,6,32,128]{3,2,1,0:T(8,128)}, f32[4,3,32,128]{3,2,1,0:T(8,128)}) custom-call(f32[3,4096]{1,0:T(4,128)} %bitcast.13, f32[1,4096]{1,0:T(1,128)} %bitcast.15, f32[1,4096]{1,0:T(1,128)} %bitcast.16, s32[1,4096]{1,0:T(1,128)} %bitcast.17, s32[1,64]{1,0:T(1,128)} %bitcast.22, f32[8]{0:T(128)} %hard.3), custom_call_target="tpu_custom_call" | custom-call | tf_op jit(solution)/shard_map/exchange/pallas_call | solution.py:263
  22.5 5.1 %pairs_sort.1 = (s32[1,1664]{1,0:T(1,128)}, s32[8,128]{1,0:T(8,128)}, f32[8,128]{1,0:T(8,128)}) custom-call(s32[1,1496]{1,0:T(1,128)} %bitcast.20, s32[1,1496]{1,0:T(1,128)} %bitcast.21, s32[1,1]{1,0:T(1,128)S(6)} %copy.20.count), custom_call_target="tpu_custom_call" | custom-call | tf_op jit(solution)/shard_map/pairs_sort/pallas_call | solution.py:73
  27.6 0.0 copy-start.4
  27.6 0.0 copy-start.6
  27.6 0.0 copy-start.7
  27.6 0.0 copy-start.8
  27.7 0.7 copy-done.4
  28.3 0.0 copy-done.6
  28.3 0.0 copy-done.7
  28.3 0.0 copy-done.8
  28.3 0.0 copy-start
  28.3 1.0 %copy-done = f32[4,6,32,128]{3,2,1,0:T(8,128)S(1)} copy-done((f32[4,6,32,128]{3,2,1,0:T(8,128)S(1)}, f32[4,6,32,128]{3,2,1,0:T(8,128)}, u32[]{:S(2)}) %copy-start) | copy-done | bytes 393240
  29.3 0.0 copy-start.1
  29.3 0.9 copy-done.1
  30.2 0.0 copy-start.3
  30.2 0.7 copy-done.3
  30.9 0.0 copy-start.5
  30.9 0.7 copy-done.5
  31.6 15.2 %pairs.1 = (f32[32,128]{1,0:T(8,128)S(1)}, f32[32,128]{1,0:T(8,128)}) custom-call(s32[1,1664]{1,0:T(1,128)S(1)} %copy-done.3, s32[8,128]{1,0:T(8,128)S(1)} %copy-done.4, f32[8]{0:T(128)S(1)} %copy-done.7, f32[8]{0:T(128)S(1)} %copy-done.8, f32[8]{0:T(128)S(1)} %copy-done.6, f32[8,128]{1,0:T(8,128)S(1)} %copy-done.5, f32[6,32,128]{2,1,0:T(8,128)S(1)} %copy-done.1, ...), custom_call_target="tpu_custom_call" | custom-call | tf_op jit(solution)/shard_map/pairs/pallas_call | solution.py:193
  46.8 0.0 copy-start.2
  46.8 0.6 copy-done.2
  47.4 46.8 %level.1 = (f32[32,128]{1,0:T(8,128)}, f32[32,128]{1,0:T(8,128)}) custom-call(f32[32,128]{1,0:T(8,128)} %copy-done.2, f32[4,3,32,128]{3,2,1,0:T(8,128)} %get-tuple-element.19.early, f32[32,128]{1,0:T(8,128)} %bitcast.14), custom_call_target="tpu_custom_call" | custom-call | tf_op jit(solution)/shard_map/level/pallas_call | solution.py:368
  94.2 0.0 copy-start.9
  94.2 1.3 %copy.21 = f32[1,1,4096]{2,1,0:T(1,128)} copy(f32[1,1,4096]{2,1,0:T(1,128)} %bitcast.19) | data formatting | bytes 32768
  95.6 0.0 copy-done.9
  95.6 0.6 copy.22
Async XLA Ops:
  27.6 0.7 copy-start.4
  27.6 0.7 copy-start.6
  27.6 0.7 copy-start.7
  27.6 0.7 copy-start.8
  28.3 1.0 %copy-start = (f32[4,6,32,128]{3,2,1,0:T(8,128)S(1)}, f32[4,6,32,128]{3,2,1,0:T(8,128)}, u32[]{:S(2)}) copy-start(f32[4,6,32,128]{3,2,1,0:T(8,128)} %get-tuple-element.17.halo) | copy-start | bytes 1179652
  29.3 0.9 copy-start.1
  30.2 0.7 copy-start.3
  30.9 0.7 copy-start.5
  46.8 0.6 copy-start.2
  94.2 1.3 %copy-start.9 = (f32[32,128]{1,0:T(8,128)S(1)}, f32[32,128]{1,0:T(8,128)}, u32[]{:S(2)}) copy-start(f32[32,128]{1,0:T(8,128)} %get-tuple-element.21) | copy-start | bytes 49156

commit v2 on v1

v2 whole, which is shorter than its diff:
```python
import functools

import jax
import jax.numpy as jnp
from jax import lax
from jax.experimental import pallas as pl
from jax.experimental.pallas import tpu as pltpu
from jax.sharding import PartitionSpec as P

F32 = jnp.float32
BF = jnp.bfloat16
HI = lax.Precision.HIGHEST
MESH = pl.DeviceIdType.MESH
kappa = 1.86

PB = 12
SB = 13
NT = 320


def order_pairs(tiles, cands, count, codes, tr, cr):
    n = tiles.shape[1]
    one = lax.broadcasted_iota(jnp.int32, (1, 128), 1)
    tr[...] = jnp.full((128, 128), 64.0, F32)
    cr[...] = jnp.zeros((16, 128), F32)
    for j in range(PB):
        w = min(128, n - 128 * j)
        tr[j : j + 1, :w] = tiles[:, 128 * j : 128 * j + w].astype(F32)
        cr[j : j + 1, :w] = cands[:, 128 * j : 128 * j + w].astype(F32)
    prow = lax.broadcasted_iota(jnp.int32, (16, 128), 0) * 128 + lax.broadcasted_iota(jnp.int32, (16, 128), 1)
    used = prow < count[0, 0]
    t = jnp.where(used, tr[:16], 64.0)
    c = jnp.where(used, cr[...], 0.0)
    tr[:16] = t
    tcol = tr[...].T
    lane = lax.broadcasted_iota(jnp.int32, (128, 128), 1)
    rowi = lax.broadcasted_iota(jnp.int32, (128, 128), 0)
    lanef = lane.astype(F32)
    before = jnp.where(lane < rowi, 1.0, 0.0).astype(BF)
    hot = [tcol[:, j : j + 1] == lanef for j in range(PB)]
    hotf = [jnp.where(h, 1.0, 0.0) for h in hot]
    sums = [jnp.sum(h, axis=0, keepdims=True) for h in hotf]
    counts = sum(sums)
    counts = jnp.where(one < 64, counts, 0.0)
    half = jnp.floor((counts + 1.0) * 0.5)
    starts = 2.0 * jnp.dot(jnp.broadcast_to(half, (8, 128)), jnp.where(rowi < lane, 1.0, 0.0), precision=HI, preferred_element_type=F32)[:1]
    starts = jnp.where(one < 64, starts, 8192.0)
    codes[:, SB * 128 :] = jnp.broadcast_to(jnp.sum(half, axis=1, keepdims=True), (1, 128)).astype(jnp.int32)
    out = jnp.zeros((8, SB * 128), F32)
    slot = lax.broadcasted_iota(jnp.int32, (128, SB * 128), 1).astype(F32)
    selfrow = jnp.zeros((1, 128), F32)
    e = float(NT) - c
    e = jnp.where(used, e, 0.0)
    ehi = jnp.floor(e * 0.5)
    elo = e - 2.0 * ehi
    same = jnp.where(t == c, 1.0, 0.0)
    r8 = lax.broadcasted_iota(jnp.int32, (8, 128), 0)
    for j in range(PB):
        rank = jnp.dot(before, hotf[j].astype(BF), preferred_element_type=F32)
        pos = jnp.sum(jnp.where(hot[j], rank + starts, 0.0), axis=1, keepdims=True)
        starts = starts + sums[j]
        vals = jnp.where(r8 == 0, ehi[j : j + 1], jnp.where(r8 == 1, elo[j : j + 1], jnp.where(r8 == 2, t[j : j + 1], same[j : j + 1])))
        put = jnp.where(pos == slot, 1.0, 0.0).astype(BF)
        out = out + jnp.dot(vals.astype(BF), put, preferred_element_type=F32)
        selfrow = selfrow + jnp.dot(vals.astype(BF), hotf[j].astype(BF), preferred_element_type=F32)[3:4]
    code = out[2:3] * 512.0 + (float(NT) - (2.0 * out[0:1] + out[1:2]))
    codes[:, : SB * 128] = code.astype(jnp.int32)
    lane32 = lax.broadcasted_iota(jnp.int32, (32, 128), 1)
    row32 = lax.broadcasted_iota(jnp.int32, (32, 128), 0)
    n = jnp.broadcast_to(selfrow, (32, 128))
    even = jnp.sum(jnp.where(lane32 == 2 * row32, n, 0.0), axis=1, keepdims=True)
    odd = jnp.sum(jnp.where(lane32 == 2 * row32 + 1, n, 0.0), axis=1, keepdims=True)
    return jnp.where(lane32 < 64, even, odd)


NR = 160
UN = 8


def pair_kernel(codes_h, widths, chi, hard, own_h, halo_h, fe, rf, codes, own, halo, sem, G, C, HB, CH, acc, FR):
    loads = [
        pltpu.make_async_copy(s, d, sem.at[k])
        for k, (s, d) in enumerate(((own_h, own), (halo_h, halo), (codes_h, codes)))
    ]
    for c in loads:
        c.start()
    lane = lax.broadcasted_iota(jnp.int32, (8, 128), 1)
    row = lax.broadcasted_iota(jnp.int32, (8, 128), 0)
    low = lane < 64
    for c in loads:
        c.wait()
    for b in range(5):
        at = [own[c] if b == 0 else halo[b - 1, c] for c in range(6)]
        if b in (1, 2):
            at[0] = at[0] + (-16.0 if b == 1 else 16.0)
        if b in (3, 4):
            at[1] = at[1] + (-32.0 if b == 3 else 32.0)
        s = jnp.zeros((32, 128), F32)
        for t in range(8):
            s = jnp.where(at[5] == float(t), widths[t], s)
        for c, x in enumerate((at[0] * 0.1, at[1] * 0.1, at[2] * 0.1, at[3] * 0.1, at[4] * 0.1, s * s * 0.01)):
            G[pl.ds(c * NR + b * 32, 32), :] = x
    G[pl.ds(6 * NR, 2 * NR), :] = jnp.zeros((2 * NR, 128), F32)

    def halves(x):
        y = pltpu.roll(x, 64, 1)
        return jnp.where(low, x, y), jnp.where(low, y, x)

    def prep(g, carry):
        c0, c1 = halves(G[pl.ds(g, 8, stride=NR), :])
        C[g * 2] = c0
        C[g * 2 + 1] = c1
        return carry

    lax.fori_loop(0, NR, prep, 0, unroll=8)
    C[NT] = jnp.where((row == 3) | (row == 4), 0.0, C[0])

    def prep_home(r, carry):
        v = G[pl.ds(r, 8, stride=NR), :]
        x = v[:, 0:1]
        y = v[:, 64:65]
        cen = jnp.where(low, jnp.broadcast_to(x, (8, 128)), jnp.broadcast_to(y, (8, 128)))
        cen = jnp.where(row < 3, cen, 0.0)
        a = v - cen
        n = jnp.sum(jnp.where(row < 3, a * a, 0.0), axis=0, keepdims=True) + 0.0025
        f = jnp.where(row < 3, -2.0 * a, jnp.where(row == 3, n, jnp.where(row == 5, a, 0.0)))
        c0, c1 = halves(cen)
        CH[r * 2] = c0
        CH[r * 2 + 1] = c1
        FR[pl.ds(pl.multiple_of(r * 8, 8), 8), :] = f
        acc[0, pl.ds(2 * r, 2)] = jnp.zeros((2, 64, 128), F32)
        acc[1, pl.ds(2 * r, 2)] = jnp.zeros((2, 64, 128), F32)
        return carry

    lax.fori_loop(0, 32, prep_home, 0, unroll=4)
    for g in range(2):
        t = FR[pl.ds(128 * g, 128), :].T
        for r in range(16):
            for k, col in enumerate((0, 1, 2, 3, 5)):
                w = jnp.broadcast_to(t[:, 8 * r + col : 8 * r + col + 1], (128, 128))
                HB[k, 32 * g + 2 * r] = w[:64]
                HB[k, 32 * g + 2 * r + 1] = w[64:]

    def step(i, carry):
        for u in range(UN):
            k1 = codes[0, 2 * UN * i + 2 * u]
            k2 = codes[0, 2 * UN * i + 2 * u + 1]
            h = lax.shift_right_logical(k1, 9)
            v = jnp.where(low, C[k1 & 511], C[k2 & 511]) - CH[h]
            n = jnp.sum(jnp.where(row < 3, v * v, 0.0), axis=0, keepdims=True)
            xs = [jnp.broadcast_to(v[k : k + 1], (8, 128)) for k in range(6)]
            n = jnp.broadcast_to(n, (8, 128))
            for q in range(8):
                rows = pl.ds(8 * q, 8)
                d = (HB[3, h, rows] + n) + HB[0, h, rows] * xs[0] + HB[1, h, rows] * xs[1] + HB[2, h, rows] * xs[2]
                w = lax.rsqrt(HB[4, h, rows] + xs[5])
                r = lax.rsqrt(d)
                e = lax.erf(d * r * w)
                m = jnp.maximum(1.0025 - d, 0.0)
                kk = (e * r) * (m * m)
                acc[0, h, rows] = acc[0, h, rows] + kk * xs[3]
                acc[1, h, rows] = acc[1, h, rows] + kk * xs[4]
        return carry

    lax.fori_loop(0, lax.div(codes[0, 1664] + UN - 1, UN), step, 0)
    def finish(r, carry):
        for f, ref in enumerate((fe, rf)):
            ref[pl.ds(r, 1), :] = jnp.sum(acc[f, pl.ds(2 * r, 2)].reshape(128, 128).T, axis=0, keepdims=True)
        return carry

    lax.fori_loop(0, 32, finish, 0, unroll=4)
    s2 = jnp.zeros((32, 128), F32)
    ch = jnp.zeros((32, 128), F32)
    eta = jnp.zeros((32, 128), F32)
    for t in range(8):
        hit = own[5] == float(t)
        s2 = jnp.where(hit, widths[t] * widths[t], s2)
        ch = jnp.where(hit, chi[t], ch)
        eta = jnp.where(hit, hard[t], eta)
    itself = own[6] * (2.0 * lax.erf(0.5 * lax.rsqrt(s2 + s2)))
    residual = rf[...] - itself * own[4]
    field = ch + (fe[...] - itself * own[3]) + residual
    rf[...] = residual
    fe[...] = field / eta


def pair_call(codes, widths, chi, hard, own, halo):
    sm = pl.BlockSpec(memory_space=pltpu.SMEM)
    vm = pl.BlockSpec(memory_space=pltpu.VMEM)
    hbm = pl.BlockSpec(memory_space=pl.ANY)
    return pl.pallas_call(
        pair_kernel,
        out_shape=[jax.ShapeDtypeStruct((32, 128), F32)] * 2,
        in_specs=[hbm] + [sm] * 3 + [hbm] * 2,
        out_specs=[vm, vm],
        scratch_shapes=[
            pltpu.SMEM(codes.shape, jnp.int32),
            pltpu.VMEM(own.shape, F32),
            pltpu.VMEM(halo.shape, F32),
            pltpu.SemaphoreType.DMA((3,)),
            pltpu.VMEM((8 * NR, 128), F32),
            pltpu.VMEM((NT + 1, 8, 128), F32),
            pltpu.VMEM((5, 64, 64, 128), F32),
            pltpu.VMEM((64, 8, 128), F32),
            pltpu.VMEM((2, 64, 64, 128), F32),
            pltpu.VMEM((256, 128), F32),
        ],
        compiler_params=pltpu.CompilerParams(vmem_limit_bytes=60 * 2**20),
        name="pairs",
    )(codes, widths, chi, hard, own, halo)


def exchange_kernel(
    pos, aux, resid, types, owner, tiles, cands, hard, count, own, halo, early, codes, send, recv, tr, cr
):
    nb, npl = lax.axis_size("brick"), lax.axis_size("plane")
    b, p = lax.axis_index("brick"), lax.axis_index("plane")
    below, above = lax.rem(b + nb - 1, nb), lax.rem(b + 1, nb)
    barrier = pltpu.get_barrier_semaphore()
    mates = [lax.rem(p + k, npl) for k in range(1, npl)]
    for d in [(below, p), (above, p)] + [(b, q) for q in mates]:
        pl.semaphore_signal(barrier, inc=1, device_id=d, device_id_type=MESH)
    for c in range(3):
        own[c] = pos[pl.ds(32 * c, 32), :]
    own[3] = aux[...]
    own[4] = resid[...]
    ty = types[...].astype(F32)
    own[5] = ty
    inverse = jnp.zeros((32, 128), F32)
    for t in range(8):
        inverse = jnp.where(ty == float(t), 1.0 / jnp.full((32, 128), hard[t], F32), inverse)
    early[p, 0:32, :] = aux[...]
    early[p, 32:64, :] = inverse
    src = lax.broadcasted_iota(jnp.int32, (64, 128), 0)
    lane = lax.broadcasted_iota(jnp.int32, (64, 128), 1) - 32 * p
    inside = (lane >= 0) & (lane < 32)
    ids = jnp.broadcast_to(owner[...].astype(F32), (8, 64))
    evens = jnp.dot(ids, jnp.where(inside & (src == 2 * lane), 1.0, 0.0), precision=HI, preferred_element_type=F32)
    odds = jnp.dot(ids, jnp.where(inside & (src == 2 * lane + 1), 1.0, 0.0), precision=HI, preferred_element_type=F32)
    r8 = lax.broadcasted_iota(jnp.int32, (8, 128), 0)
    early[p, 64:72, :] = jnp.where(r8 == 0, evens, odds)
    pl.semaphore_wait(barrier, 1 + npl)

    def copy(s, d, k, to):
        return pltpu.make_async_remote_copy(
            src_ref=s, dst_ref=d, send_sem=send.at[k], recv_sem=recv.at[k], device_id=to, device_id_type=MESH
        )

    left, right = lax.rem(p + npl - 1, npl), lax.rem(p + 1, npl)
    mine = own.at[pl.ds(0, 6)]
    copies = [
        copy(mine, halo.at[0], 0, (above, p)),
        copy(mine, halo.at[1], 1, (below, p)),
        copy(mine, halo.at[2], 2, (b, right)),
        copy(mine, halo.at[3], 3, (b, left)),
    ] + [copy(early.at[p], early.at[p], 4 + k, (b, q)) for k, q in enumerate(mates)]
    for c in copies:
        c.start()
    own[6] = order_pairs(tiles, cands, count, codes, tr, cr)
    for c in copies:
        c.wait()


def exchange(pos, aux, resid, types, owner, tiles, cands, hard, count):
    vm = pl.BlockSpec(memory_space=pltpu.VMEM)
    return pl.pallas_call(
        exchange_kernel,
        out_shape=[
            jax.ShapeDtypeStruct((7, 32, 128), F32),
            jax.ShapeDtypeStruct((4, 6, 32, 128), F32),
            jax.ShapeDtypeStruct((4, 72, 128), F32),
            jax.ShapeDtypeStruct((1, (SB + 1) * 128), jnp.int32),
        ],
        in_specs=[vm] * 7 + [pl.BlockSpec(memory_space=pltpu.SMEM)] * 2,
        out_specs=[vm] * 4,
        scratch_shapes=[
            pltpu.SemaphoreType.DMA((7,)),
            pltpu.SemaphoreType.DMA((7,)),
            pltpu.VMEM((128, 128), F32),
            pltpu.VMEM((16, 128), F32),
        ],
        compiler_params=pltpu.CompilerParams(collective_id=0, has_side_effects=True),
        name="exchange",
    )(pos, aux, resid, types, owner, tiles, cands, hard, count)


LINE, SHEET = 16, 32


def level_kernel(fe, early, prev, charges, nxt, got, near, far, s1, r1, s2, r2, s3, r3):
    npl = lax.axis_size("plane")
    b, p = lax.axis_index("brick"), lax.axis_index("plane")
    zhi = lax.rem(lax.div(b, 8), 4)
    z = npl * zhi + p
    w = 8 * lax.div(b, 32) + lax.rem(b, 8)

    def line(q):
        return (b + 8 * (lax.div(q, npl) - zhi), lax.rem(q, npl))

    def sheet(q):
        return (32 * lax.div(q, 8) + 8 * zhi + lax.rem(q, 8), p)

    lines = [lax.rem(z + k, LINE) for k in range(1, LINE)]
    sheets = [lax.rem(w + k, SHEET) for k in range(1, SHEET)]
    mates = [lax.rem(p + k, npl) for k in range(1, npl)]
    barrier = pltpu.get_barrier_semaphore()
    for q in lines:
        pl.semaphore_signal(barrier, inc=1, device_id=line(q), device_id_type=MESH)
    for q in sheets:
        pl.semaphore_signal(barrier, inc=1, device_id=sheet(q), device_id_type=MESH)
    got[p] = fe[...]

    def fold(x):
        s = x[0:8] + x[8:16] + x[16:24] + x[24:32]
        return s[0:4] + s[4:8]

    near[w] = jnp.concatenate([fold(early[p, 0:32, :] + fe[...]), fold(early[p, 32:64, :])], axis=0)
    pl.semaphore_wait(barrier, LINE + SHEET - 2)

    def copy(s, d, ss, rs, to):
        return pltpu.make_async_remote_copy(
            src_ref=s, dst_ref=d, send_sem=ss, recv_sem=rs, device_id=to, device_id_type=MESH
        )

    first = [copy(near.at[w], near.at[w], s1.at[k], r1.at[k], sheet(q)) for k, q in enumerate(sheets)]
    for c in first:
        c.start()
    tiles = [copy(got.at[p], got.at[p], s2.at[k], r2.at[k], (b, q)) for k, q in enumerate(mates)]
    for c in tiles:
        c.start()
    evens = early[0, 64:65, :] + early[1, 64:65, :] + early[2, 64:65, :] + early[3, 64:65, :]
    odds = early[0, 65:66, :] + early[1, 65:66, :] + early[2, 65:66, :] + early[3, 65:66, :]
    slot = (64 * p + 2 * lax.broadcasted_iota(jnp.int32, (32, 128), 0)).astype(F32)
    place = jnp.concatenate(
        [
            jnp.where(evens == slot, 1.0, 0.0),
            jnp.where(odds == slot + 1.0, 1.0, 0.0),
            jnp.where(evens == slot + 1.0, 1.0, 0.0),
            jnp.where(odds == slot, 1.0, 0.0),
        ],
        axis=0,
    )
    low = lax.broadcasted_iota(jnp.int32, (32, 128), 1) < 64

    def placed(x):
        y = jnp.dot(place, x, precision=HI, preferred_element_type=F32)
        return jnp.where(low, y[0:32], y[32:64]) + pltpu.roll(jnp.where(low, y[64:96], y[96:128]), 64, 1)

    aux = placed(early[:, 0:32, :].reshape(128, 128))
    inverse = placed(early[:, 32:64, :].reshape(128, 128))
    for c in first:
        c.wait()
    total = near[0]
    for k in range(1, SHEET):
        total = total + near[k]
    far[z] = total
    second = [copy(far.at[z], far.at[z], s3.at[k], r3.at[k], line(q)) for k, q in enumerate(lines)]
    for c in second:
        c.start()
    for c in tiles:
        c.wait()
    moved = placed(got[...].reshape(128, 128))
    for c in second:
        c.wait()
    total = far[0]
    for k in range(1, LINE):
        total = total + far[k]
    top = jnp.sum(jnp.sum(total[0:4], axis=1, keepdims=True), axis=0, keepdims=True)
    bottom = jnp.sum(jnp.sum(total[4:8], axis=1, keepdims=True), axis=0, keepdims=True)
    level = jnp.broadcast_to(top / bottom, (32, 128))
    charges[...] = level * early[p, 32:64, :] - fe[...]
    nxt[...] = 2.0 * aux - prev[...] + kappa * (level * inverse - moved - aux)


def finish(fe, early, prev):
    vm = pl.BlockSpec(memory_space=pltpu.VMEM)
    dma = pltpu.SemaphoreType.DMA
    return pl.pallas_call(
        level_kernel,
        out_shape=[jax.ShapeDtypeStruct((32, 128), F32)] * 2,
        in_specs=[vm] * 3,
        out_specs=[vm] * 2,
        scratch_shapes=[
            pltpu.VMEM((4, 32, 128), F32),
            pltpu.VMEM((SHEET, 8, 128), F32),
            pltpu.VMEM((LINE, 8, 128), F32),
            dma((SHEET - 1,)), dma((SHEET - 1,)), dma((3,)), dma((3,)), dma((LINE - 1,)), dma((LINE - 1,)),
        ],
        compiler_params=pltpu.CompilerParams(collective_id=1, has_side_effects=True),
        name="level",
    )(fe, early, prev)


def on_device(positions, aux, aux_prev, resid, types, pair_tiles, pair_cands, pair_count, owner_tile, electroneg, hardness, widths):
    own, halo, early, codes = exchange(
        positions.transpose(0, 2, 1, 3).reshape(96, 128),
        aux.reshape(32, 128),
        resid.reshape(32, 128),
        types.reshape(32, 128),
        owner_tile.reshape(1, -1),
        pair_tiles.reshape(1, -1),
        pair_cands.reshape(1, -1),
        hardness,
        pair_count,
    )
    fe, rf = pair_call(codes, widths, electroneg, hardness, own, halo)
    charges, nxt = finish(fe, early, aux_prev.reshape(32, 128))
    return charges.reshape(aux.shape), nxt.reshape(aux.shape), rf.reshape(aux.shape)


def solution(mesh):
    s4, s3, s2 = P("brick", "plane", None, None), P("brick", "plane", None), P("brick", "plane")
    return jax.shard_map(
        on_device,
        mesh=mesh,
        in_specs=(s4, s3, s3, s3, s3, s3, s3, s2, s3, P(), P(), P()),
        out_specs=(s3, s3, s3),
        check_vma=False,
    )
```

time: 96.8 us -> 82.9 us (0.86)
  Pallas kernels: 86.9 us -> 79.3 us
  local copies, waits for them, and re-layouts: 7.96 us -> 1.94 us
    unnamed x23 -> x4, local copies, waits for them, and re-layouts: 7.96 us -> 1.94 us
    pallas_call x2 -> x1, Pallas kernels: 24.9 us -> 19.8 us  [exchange(): pl.pallas_call(exchange_kernel, out_shape=[jax.ShapeDtypeStruct((7, 32, 1...]
    pallas_call x1, Pallas kernels: 46.8 us -> 42.2 us  [finish(): pl.pallas_call(level_kernel, out_shape=[jax.ShapeDtypeStruct((32, 128), F...]
    pallas_call x1, Pallas kernels: 15.2 us -> 17.3 us  [pair_call(): pl.pallas_call(pair_kernel, out_shape=[jax.ShapeDtypeStruct((32, 128), F3...]
where the time goes in v2:
time: 82.9 us; the launch traced here: 82.6 us
  Pallas kernels  79.3 us (96%)
  local copies, waits for them, and re-layouts  1.94 us (2%)
  between operations  1.31 us (2%)
    pallas_call x1, Pallas kernels, finish(): pl.pallas_call(level_kernel, out_shape=[jax.ShapeDtypeStruct((32, 128), F...  42.2 us
    pallas_call x1, Pallas kernels, exchange(): pl.pallas_call(exchange_kernel, out_shape=[jax.ShapeDtypeStruct((7, 32, 1...  19.8 us
    pallas_call x1, Pallas kernels, pair_call(): pl.pallas_call(pair_kernel, out_shape=[jax.ShapeDtypeStruct((32, 128), F3...  17.3 us
    unnamed x4, local copies, waits for them, and re-layouts  1.94 us

profile of v2, /device:TPU:1, one launch (start us, length us, event | category | flops | bytes accessed | tf_op | source)
XLA Modules:
  0.0 82.6 jit_solution(14866553785045802296)
XLA Ops:
  1.3 19.8 %exchange.1 = (f32[7,32,128]{2,1,0:T(8,128)}, f32[4,6,32,128]{3,2,1,0:T(8,128)}, f32[4,72,128]{2,1,0:T(8,128)}, s32[1,1792]{1,0:T(1,128)}) custom-call(f32[96,128]{1,0:T(8,128)} %bitcast.11, f32[32,128]{1,0:T(8,128)} %bitcast.12, f32[32,128]{1,0:T(8,128)} %bitcast.13, s32[32,128]{1,0:T(8,128)} %bitcast.14, s32[1,64]{1,0:T(1,128)} %bitcast.20, ...), custom_call_target="tpu_custom_call" | custom-call | tf_op jit(solution)/shard_map/exchange/pallas_call | solution.py:266
  21.1 17.3 %pairs.1 = (f32[32,128]{1,0:T(8,128)}, f32[32,128]{1,0:T(8,128)}) custom-call(s32[1,1792]{1,0:T(1,128)} %get-tuple-element.11.codes_h, f32[8]{0:T(128)} %widths.1, f32[8]{0:T(128)} %chi.1, f32[8]{0:T(128)} %hard.3, f32[7,32,128]{2,1,0:T(8,128)} %get-tuple-element.12.own_h, f32[4,6,32,128]{3,2,1,0:T(8,128)} %get-tuple-element.13.halo_h), custom_call_target="tpu_custom_call" | custom-call | tf_op jit(solution)/shard_map/pairs/pallas_call | solution.py:191
  38.4 42.2 %level.1 = (f32[32,128]{1,0:T(8,128)}, f32[32,128]{1,0:T(8,128)}) custom-call(f32[32,128]{1,0:T(8,128)} %get-tuple-element.14.fe, f32[4,72,128]{2,1,0:T(8,128)} %get-tuple-element.15.early, f32[32,128]{1,0:T(8,128)} %bitcast.17), custom_call_target="tpu_custom_call" | custom-call | tf_op jit(solution)/shard_map/level/pallas_call | solution.py:378
  80.6 0.0 copy-start
  80.7 1.3 %copy.18 = f32[1,1,4096]{2,1,0:T(1,128)} copy(f32[1,1,4096]{2,1,0:T(1,128)} %bitcast.16) | data formatting | bytes 32768
  82.0 0.0 copy-done
  82.0 0.6 copy.19
Async XLA Ops:
  80.6 1.3 %copy-start = (f32[32,128]{1,0:T(8,128)S(1)}, f32[32,128]{1,0:T(8,128)}, u32[]{:S(2)}) copy-start(f32[32,128]{1,0:T(8,128)} %get-tuple-element.17) | copy-start | bytes 49156

commit v3 on v2

--- a/solution.py
+++ b/solution.py
@@ -75,9 +75,17 @@
 
 NR = 160
 UN = 8
-
-
-def pair_kernel(codes_h, widths, chi, hard, own_h, halo_h, fe, rf, codes, own, halo, sem, G, C, HB, CH, acc, FR):
+NB = 2
+
+
+def split3(x):
+    a = x.astype(BF).astype(F32)
+    r = x - a
+    b = r.astype(BF).astype(F32)
+    return a, b, r - b
+
+
+def pair_kernel(codes_h, widths, chi, hard, own_h, halo_h, fe, rf, codes, own, halo, sem, G, C, HS, CH, acc, FR, L, *bufs):
     loads = [
         pltpu.make_async_copy(s, d, sem.at[k])
         for k, (s, d) in enumerate(((own_h, own), (halo_h, halo), (codes_h, codes)))
@@ -101,6 +109,10 @@
         for c, x in enumerate((at[0] * 0.1, at[1] * 0.1, at[2] * 0.1, at[3] * 0.1, at[4] * 0.1, s * s * 0.01)):
             G[pl.ds(c * NR + b * 32, 32), :] = x
     G[pl.ds(6 * NR, 2 * NR), :] = jnp.zeros((2 * NR, 128), F32)
+    DS, VS = bufs[:NB], bufs[NB:]
+    for k in range(NB):
+        DS[k][...] = jnp.ones_like(DS[k])
+        VS[k][...] = jnp.zeros_like(VS[k])
 
     def halves(x):
         y = pltpu.roll(x, 64, 1)
@@ -123,46 +135,63 @@
         cen = jnp.where(row < 3, cen, 0.0)
         a = v - cen
         n = jnp.sum(jnp.where(row < 3, a * a, 0.0), axis=0, keepdims=True) + 0.0025
-        f = jnp.where(row < 3, -2.0 * a, jnp.where(row == 3, n, jnp.where(row == 5, a, 0.0)))
+        f = jnp.where(row < 3, -2.0 * a, jnp.where(row < 6, 1.0, jnp.where(row == 6, n, 0.0)))
+        f1, f2, f3 = split3(f)
+        t = jnp.concatenate([f1, f1, f1, f2, f2, f3, jnp.zeros((80, 128), F32)], axis=0).T.astype(BF)
+        L[r * 2] = t[:64]
+        L[r * 2 + 1] = t[64:]
         c0, c1 = halves(cen)
         CH[r * 2] = c0
         CH[r * 2 + 1] = c1
-        FR[pl.ds(pl.multiple_of(r * 8, 8), 8), :] = f
+        FR[pl.ds(r, 1), :] = v[5:6, :]
         acc[0, pl.ds(2 * r, 2)] = jnp.zeros((2, 64, 128), F32)
         acc[1, pl.ds(2 * r, 2)] = jnp.zeros((2, 64, 128), F32)
         return carry
 
     lax.fori_loop(0, 32, prep_home, 0, unroll=4)
-    for g in range(2):
-        t = FR[pl.ds(128 * g, 128), :].T
-        for r in range(16):
-            for k, col in enumerate((0, 1, 2, 3, 5)):
-                w = jnp.broadcast_to(t[:, 8 * r + col : 8 * r + col + 1], (128, 128))
-                HB[k, 32 * g + 2 * r] = w[:64]
-                HB[k, 32 * g + 2 * r + 1] = w[64:]
-
-    def step(i, carry):
+    t = FR[...].T
+    for r in range(32):
+        w = jnp.broadcast_to(t[:, r : r + 1], (128, 128))
+        HS[2 * r] = w[:64]
+        HS[2 * r + 1] = w[64:]
+    last = jnp.where(row == 6, 1.0, 0.0)
+
+    def terms(i, D, V):
+        for u in range(UN):
+            h = lax.shift_right_logical(codes[0, 2 * UN * i + 2 * u], 9)
+            xs = [jnp.broadcast_to(V[u, k : k + 1], (8, 128)) for k in range(3, 6)]
+            for q in range(8):
+                rows = pl.ds(8 * q, 8)
+                d = D[u, rows]
+                w = lax.rsqrt(HS[h, rows] + xs[2])
+                r = lax.rsqrt(d)
+                e = lax.erf(d * r * w)
+                m = jnp.maximum(1.0025 - d, 0.0)
+                kk = (e * r) * (m * m)
+                acc[0, h, rows] = acc[0, h, rows] + kk * xs[0]
+                acc[1, h, rows] = acc[1, h, rows] + kk * xs[1]
+
+    def distances(i, D, V):
         for u in range(UN):
             k1 = codes[0, 2 * UN * i + 2 * u]
             k2 = codes[0, 2 * UN * i + 2 * u + 1]
             h = lax.shift_right_logical(k1, 9)
             v = jnp.where(low, C[k1 & 511], C[k2 & 511]) - CH[h]
-            n = jnp.sum(jnp.where(row < 3, v * v, 0.0), axis=0, keepdims=True)
-            xs = [jnp.broadcast_to(v[k : k + 1], (8, 128)) for k in range(6)]
-            n = jnp.broadcast_to(n, (8, 128))
-            for q in range(8):
-                rows = pl.ds(8 * q, 8)
-                d = (HB[3, h, rows] + n) + HB[0, h, rows] * xs[0] + HB[1, h, rows] * xs[1] + HB[2, h, rows] * xs[2]
-                w = lax.rsqrt(HB[4, h, rows] + xs[5])
-                r = lax.rsqrt(d)
-                e = lax.erf(d * r * w)
-                m = jnp.maximum(1.0025 - d, 0.0)
-                kk = (e * r) * (m * m)
-                acc[0, h, rows] = acc[0, h, rows] + kk * xs[3]
-                acc[1, h, rows] = acc[1, h, rows] + kk * xs[4]
+            V[u] = v
+            f = jnp.where(row < 3, v, jnp.where(row < 6, pltpu.roll(v * v, 3, 0), last))
+            s1, s2, s3 = split3(f)
+            g = jnp.concatenate([s1, s2, s3, s1, s2, s1], axis=0).astype(BF)
+            D[u] = jnp.dot(L[h, :, pl.ds(0, 48)], g, preferred_element_type=F32)
+
+    def step(i, carry):
+        for k in range(NB):
+            terms(jnp.maximum(NB * i + k - 1, 0), DS[k - 1], VS[k - 1])
+            distances(NB * i + k, DS[k], VS[k])
         return carry
 
-    lax.fori_loop(0, lax.div(codes[0, 1664] + UN - 1, UN), step, 0)
+    blocks = lax.div(codes[0, 1664] + UN - 1, UN)
+    lax.fori_loop(0, lax.div(blocks + NB, NB), step, 0)
+
     def finish(r, carry):
         for f, ref in enumerate((fe, rf)):
             ref[pl.ds(r, 1), :] = jnp.sum(acc[f, pl.ds(2 * r, 2)].reshape(128, 128).T, axis=0, keepdims=True)
@@ -200,10 +229,13 @@
             pltpu.SemaphoreType.DMA((3,)),
             pltpu.VMEM((8 * NR, 128), F32),
             pltpu.VMEM((NT + 1, 8, 128), F32),
-            pltpu.VMEM((5, 64, 64, 128), F32),
+            pltpu.VMEM((64, 64, 128), F32),
             pltpu.VMEM((64, 8, 128), F32),
             pltpu.VMEM((2, 64, 64, 128), F32),
-            pltpu.VMEM((256, 128), F32),
+            pltpu.VMEM((128, 128), F32),
+            pltpu.VMEM((64, 64, 128), BF),
+            *[pltpu.VMEM((UN, 64, 128), F32)] * NB,
+            *[pltpu.VMEM((UN, 8, 128), F32)] * NB,
         ],
         compiler_params=pltpu.CompilerParams(vmem_limit_bytes=60 * 2**20),
         name="pairs",
@@ -217,8 +249,8 @@
     b, p = lax.axis_index("brick"), lax.axis_index("plane")
     below, above = lax.rem(b + nb - 1, nb), lax.rem(b + 1, nb)
     barrier = pltpu.get_barrier_semaphore()
-    mates = [lax.rem(p + k, npl) for k in range(1, npl)]
-    for d in [(below, p), (above, p)] + [(b, q) for q in mates]:
+    left, right = lax.rem(p + npl - 1, npl), lax.rem(p + 1, npl)
+    for d in [(below, p), (above, p), (b, left), (b, right)]:
         pl.semaphore_signal(barrier, inc=1, device_id=d, device_id_type=MESH)
     for c in range(3):
         own[c] = pos[pl.ds(32 * c, 32), :]
@@ -229,8 +261,8 @@
     inverse = jnp.zeros((32, 128), F32)
     for t in range(8):
         inverse = jnp.where(ty == float(t), 1.0 / jnp.full((32, 128), hard[t], F32), inverse)
-    early[p, 0:32, :] = aux[...]
-    early[p, 32:64, :] = inverse
+    early[0:32, :] = aux[...]
+    early[32:64, :] = inverse
     src = lax.broadcasted_iota(jnp.int32, (64, 128), 0)
     lane = lax.broadcasted_iota(jnp.int32, (64, 128), 1) - 32 * p
     inside = (lane >= 0) & (lane < 32)
@@ -238,22 +270,21 @@
     evens = jnp.dot(ids, jnp.where(inside & (src == 2 * lane), 1.0, 0.0), precision=HI, preferred_element_type=F32)
     odds = jnp.dot(ids, jnp.where(inside & (src == 2 * lane + 1), 1.0, 0.0), precision=HI, preferred_element_type=F32)
     r8 = lax.broadcasted_iota(jnp.int32, (8, 128), 0)
-    early[p, 64:72, :] = jnp.where(r8 == 0, evens, odds)
-    pl.semaphore_wait(barrier, 1 + npl)
+    early[64:72, :] = jnp.where(r8 == 0, evens, odds)
+    pl.semaphore_wait(barrier, 4)
 
     def copy(s, d, k, to):
         return pltpu.make_async_remote_copy(
             src_ref=s, dst_ref=d, send_sem=send.at[k], recv_sem=recv.at[k], device_id=to, device_id_type=MESH
         )
 
-    left, right = lax.rem(p + npl - 1, npl), lax.rem(p + 1, npl)
     mine = own.at[pl.ds(0, 6)]
     copies = [
         copy(mine, halo.at[0], 0, (above, p)),
         copy(mine, halo.at[1], 1, (below, p)),
         copy(mine, halo.at[2], 2, (b, right)),
         copy(mine, halo.at[3], 3, (b, left)),
-    ] + [copy(early.at[p], early.at[p], 4 + k, (b, q)) for k, q in enumerate(mates)]
+    ]
     for c in copies:
         c.start()
     own[6] = order_pairs(tiles, cands, count, codes, tr, cr)
@@ -268,14 +299,14 @@
         out_shape=[
             jax.ShapeDtypeStruct((7, 32, 128), F32),
             jax.ShapeDtypeStruct((4, 6, 32, 128), F32),
-            jax.ShapeDtypeStruct((4, 72, 128), F32),
+            jax.ShapeDtypeStruct((72, 128), F32),
             jax.ShapeDtypeStruct((1, (SB + 1) * 128), jnp.int32),
         ],
         in_specs=[vm] * 7 + [pl.BlockSpec(memory_space=pltpu.SMEM)] * 2,
         out_specs=[vm] * 4,
         scratch_shapes=[
-            pltpu.SemaphoreType.DMA((7,)),
-            pltpu.SemaphoreType.DMA((7,)),
+            pltpu.SemaphoreType.DMA((4,)),
+            pltpu.SemaphoreType.DMA((4,)),
             pltpu.VMEM((128, 128), F32),
             pltpu.VMEM((16, 128), F32),
         ],
@@ -308,13 +339,14 @@
         pl.semaphore_signal(barrier, inc=1, device_id=line(q), device_id_type=MESH)
     for q in sheets:
         pl.semaphore_signal(barrier, inc=1, device_id=sheet(q), device_id_type=MESH)
-    got[p] = fe[...]
+    got[p, 0:72, :] = early[...]
+    got[p, 72:104, :] = fe[...]
 
     def fold(x):
         s = x[0:8] + x[8:16] + x[16:24] + x[24:32]
         return s[0:4] + s[4:8]
 
-    near[w] = jnp.concatenate([fold(early[p, 0:32, :] + fe[...]), fold(early[p, 32:64, :])], axis=0)
+    near[w] = jnp.concatenate([fold(early[0:32, :] + fe[...]), fold(early[32:64, :])], axis=0)
     pl.semaphore_wait(barrier, LINE + SHEET - 2)
 
     def copy(s, d, ss, rs, to):
@@ -328,8 +360,19 @@
     tiles = [copy(got.at[p], got.at[p], s2.at[k], r2.at[k], (b, q)) for k, q in enumerate(mates)]
     for c in tiles:
         c.start()
-    evens = early[0, 64:65, :] + early[1, 64:65, :] + early[2, 64:65, :] + early[3, 64:65, :]
-    odds = early[0, 65:66, :] + early[1, 65:66, :] + early[2, 65:66, :] + early[3, 65:66, :]
+    for c in first:
+        c.wait()
+    total = near[0]
+    for k in range(1, SHEET):
+        total = total + near[k]
+    far[z] = total
+    second = [copy(far.at[z], far.at[z], s3.at[k], r3.at[k], line(q)) for k, q in enumerate(lines)]
+    for c in second:
+        c.start()
+    for c in tiles:
+        c.wait()
+    evens = got[0, 64:65, :] + got[1, 64:65, :] + got[2, 64:65, :] + got[3, 64:65, :]
+    odds = got[0, 65:66, :] + got[1, 65:66, :] + got[2, 65:66, :] + got[3, 65:66, :]
     slot = (64 * p + 2 * lax.broadcasted_iota(jnp.int32, (32, 128), 0)).astype(F32)
     place = jnp.concatenate(
         [
@@ -346,20 +389,9 @@
         y = jnp.dot(place, x, precision=HI, preferred_element_type=F32)
         return jnp.where(low, y[0:32], y[32:64]) + pltpu.roll(jnp.where(low, y[64:96], y[96:128]), 64, 1)
 
-    aux = placed(early[:, 0:32, :].reshape(128, 128))
-    inverse = placed(early[:, 32:64, :].reshape(128, 128))
-    for c in first:
-        c.wait()
-    total = near[0]
-    for k in range(1, SHEET):
-        total = total + near[k]
-    far[z] = total
-    second = [copy(far.at[z], far.at[z], s3.at[k], r3.at[k], line(q)) for k, q in enumerate(lines)]
-    for c in second:
-        c.start()
-    for c in tiles:
-        c.wait()
-    moved = placed(got[...].reshape(128, 128))
+    aux = placed(got[:, 0:32, :].reshape(128, 128))
+    inverse = placed(got[:, 32:64, :].reshape(128, 128))
+    moved = placed(got[:, 72:104, :].reshape(128, 128))
     for c in second:
         c.wait()
     total = far[0]
@@ -368,7 +400,7 @@
     top = jnp.sum(jnp.sum(total[0:4], axis=1, keepdims=True), axis=0, keepdims=True)
     bottom = jnp.sum(jnp.sum(total[4:8], axis=1, keepdims=True), axis=0, keepdims=True)
     level = jnp.broadcast_to(top / bottom, (32, 128))
-    charges[...] = level * early[p, 32:64, :] - fe[...]
+    charges[...] = level * early[32:64, :] - fe[...]
     nxt[...] = 2.0 * aux - prev[...] + kappa * (level * inverse - moved - aux)
 
 
@@ -381,7 +413,7 @@
         in_specs=[vm] * 3,
         out_specs=[vm] * 2,
         scratch_shapes=[
-            pltpu.VMEM((4, 32, 128), F32),
+            pltpu.VMEM((4, 104, 128), F32),
             pltpu.VMEM((SHEET, 8, 128), F32),
             pltpu.VMEM((LINE, 8, 128), F32),
             dma((SHEET - 1,)), dma((SHEET - 1,)), dma((3,)), dma((3,)), dma((LINE - 1,)), dma((LINE - 1,)),

time: 82.9 us -> 76.7 us (0.925)
  Pallas kernels: 79.3 us -> 72.9 us
    pallas_call x1, Pallas kernels: 42.2 us -> 38.9 us  [finish(): pl.pallas_call(level_kernel, out_shape=[jax.ShapeDtypeStruct((32, 128), F...]
    pallas_call x1, Pallas kernels: 17.3 us -> 14.4 us  [pair_call(): pl.pallas_call(pair_kernel, out_shape=[jax.ShapeDtypeStruct((32, 128), F3...]
where the time goes in v3:
time: 76.7 us; the launch traced here: 76.2 us
  Pallas kernels  72.9 us (95%)
  local copies, waits for them, and re-layouts  1.94 us (3%)
  between operations  1.31 us (2%)
    pallas_call x1, Pallas kernels, finish(): pl.pallas_call(level_kernel, out_shape=[jax.ShapeDtypeStruct((32, 128), F...  38.9 us
    pallas_call x1, Pallas kernels, exchange(): pl.pallas_call(exchange_kernel, out_shape=[jax.ShapeDtypeStruct((7, 32, 1...  19.7 us
    pallas_call x1, Pallas kernels, pair_call(): pl.pallas_call(pair_kernel, out_shape=[jax.ShapeDtypeStruct((32, 128), F3...  14.4 us
    unnamed x4, local copies, waits for them, and re-layouts  1.94 us

profile of v3, /device:TPU:1, one launch (start us, length us, event | category | flops | bytes accessed | tf_op | source)
XLA Modules:
  0.0 76.2 jit_solution(15131112980381186395)
XLA Ops:
  1.3 19.7 %exchange.1 = (f32[7,32,128]{2,1,0:T(8,128)}, f32[4,6,32,128]{3,2,1,0:T(8,128)}, f32[72,128]{1,0:T(8,128)}, s32[1,1792]{1,0:T(1,128)}) custom-call(f32[96,128]{1,0:T(8,128)} %bitcast.11, f32[32,128]{1,0:T(8,128)} %bitcast.12, f32[32,128]{1,0:T(8,128)} %bitcast.13, s32[32,128]{1,0:T(8,128)} %bitcast.14, s32[1,64]{1,0:T(1,128)} %bitcast.20, ...), custom_call_target="tpu_custom_call" | custom-call | tf_op jit(solution)/shard_map/exchange/pallas_call | solution.py:297
  21.0 14.4 %pairs.1 = (f32[32,128]{1,0:T(8,128)}, f32[32,128]{1,0:T(8,128)}) custom-call(s32[1,1792]{1,0:T(1,128)} %get-tuple-element.11.codes_h, f32[8]{0:T(128)} %widths.1, f32[8]{0:T(128)} %chi.1, f32[8]{0:T(128)} %hard.3, f32[7,32,128]{2,1,0:T(8,128)} %get-tuple-element.12.own_h, f32[4,6,32,128]{3,2,1,0:T(8,128)} %get-tuple-element.13.halo_h), custom_call_target="tpu_custom_call" | custom-call | tf_op jit(solution)/shard_map/pairs/pallas_call | solution.py:220
  35.4 38.9 %level.1 = (f32[32,128]{1,0:T(8,128)}, f32[32,128]{1,0:T(8,128)}) custom-call(f32[32,128]{1,0:T(8,128)} %get-tuple-element.14.fe, f32[72,128]{1,0:T(8,128)} %get-tuple-element.15.early, f32[32,128]{1,0:T(8,128)} %bitcast.15), custom_call_target="tpu_custom_call" | custom-call | tf_op jit(solution)/shard_map/level/pallas_call | solution.py:410
  74.2 0.0 copy-start
  74.2 1.3 %copy.18 = f32[1,1,4096]{2,1,0:T(1,128)} copy(f32[1,1,4096]{2,1,0:T(1,128)} %bitcast.17) | data formatting | bytes 32768
  75.6 0.0 copy-done
  75.6 0.6 copy.19
Async XLA Ops:
  74.2 1.3 %copy-start = (f32[32,128]{1,0:T(8,128)S(1)}, f32[32,128]{1,0:T(8,128)}, u32[]{:S(2)}) copy-start(f32[32,128]{1,0:T(8,128)} %get-tuple-element.17) | copy-start | bytes 49156

commit v4 on v3

--- a/solution.py
+++ b/solution.py
@@ -85,7 +85,7 @@
     return a, b, r - b
 
 
-def pair_kernel(codes_h, widths, chi, hard, own_h, halo_h, fe, rf, codes, own, halo, sem, G, C, HS, CH, acc, FR, L, *bufs):
+def pair_kernel(codes_h, widths, chi, hard, own_h, halo_h, fe, rf, codes, own, halo, sem, G, C, CH, acc, L, *bufs):
     loads = [
         pltpu.make_async_copy(s, d, sem.at[k])
         for k, (s, d) in enumerate(((own_h, own), (halo_h, halo), (codes_h, codes)))
@@ -103,10 +103,7 @@
             at[0] = at[0] + (-16.0 if b == 1 else 16.0)
         if b in (3, 4):
             at[1] = at[1] + (-32.0 if b == 3 else 32.0)
-        s = jnp.zeros((32, 128), F32)
-        for t in range(8):
-            s = jnp.where(at[5] == float(t), widths[t], s)
-        for c, x in enumerate((at[0] * 0.1, at[1] * 0.1, at[2] * 0.1, at[3] * 0.1, at[4] * 0.1, s * s * 0.01)):
+        for c, x in enumerate((at[0] * 0.1, at[1] * 0.1, at[2] * 0.1, at[3] * 0.1, at[4] * 0.1, at[5])):
             G[pl.ds(c * NR + b * 32, 32), :] = x
     G[pl.ds(6 * NR, 2 * NR), :] = jnp.zeros((2 * NR, 128), F32)
     DS, VS = bufs[:NB], bufs[NB:]
@@ -124,8 +121,13 @@
         C[g * 2 + 1] = c1
         return carry
 
-    lax.fori_loop(0, NR, prep, 0, unroll=8)
+    lax.fori_loop(0, NR, prep, 0, unroll=16)
     C[NT] = jnp.where((row == 3) | (row == 4), 0.0, C[0])
+
+    st = jnp.zeros((8, 128), F32)
+    for t in range(8):
+        st = jnp.where(row == t, widths[t], st)
+    st = st * st * 0.01
 
     def prep_home(r, carry):
         v = G[pl.ds(r, 8, stride=NR), :]
@@ -137,33 +139,32 @@
         n = jnp.sum(jnp.where(row < 3, a * a, 0.0), axis=0, keepdims=True) + 0.0025
         f = jnp.where(row < 3, -2.0 * a, jnp.where(row < 6, 1.0, jnp.where(row == 6, n, 0.0)))
         f1, f2, f3 = split3(f)
-        t = jnp.concatenate([f1, f1, f1, f2, f2, f3, jnp.zeros((80, 128), F32)], axis=0).T.astype(BF)
+        si = jnp.sum(jnp.where(row.astype(F32) == v[5:6], st, 0.0), axis=0, keepdims=True)
+        w1, w2, w3 = split3(lax.rsqrt(st + si))
+        t = jnp.concatenate([f1, f1, f1, f2, f2, f3, w1, w2, jnp.zeros((64, 128), F32)], axis=0).T.astype(BF)
         L[r * 2] = t[:64]
         L[r * 2 + 1] = t[64:]
         c0, c1 = halves(cen)
         CH[r * 2] = c0
         CH[r * 2 + 1] = c1
-        FR[pl.ds(r, 1), :] = v[5:6, :]
         acc[0, pl.ds(2 * r, 2)] = jnp.zeros((2, 64, 128), F32)
         acc[1, pl.ds(2 * r, 2)] = jnp.zeros((2, 64, 128), F32)
         return carry
 
-    lax.fori_loop(0, 32, prep_home, 0, unroll=4)
-    t = FR[...].T
-    for r in range(32):
-        w = jnp.broadcast_to(t[:, r : r + 1], (128, 128))
-        HS[2 * r] = w[:64]
-        HS[2 * r + 1] = w[64:]
+    lax.fori_loop(0, 32, prep_home, 0, unroll=8)
+    types8 = row.astype(F32)
+    zeros16 = jnp.zeros((16, 128), BF)
+    zeros48 = jnp.zeros((48, 128), BF)
     last = jnp.where(row == 6, 1.0, 0.0)
 
     def terms(i, D, V):
         for u in range(UN):
             h = lax.shift_right_logical(codes[0, 2 * UN * i + 2 * u], 9)
-            xs = [jnp.broadcast_to(V[u, k : k + 1], (8, 128)) for k in range(3, 6)]
+            xs = [jnp.broadcast_to(V[u, k : k + 1], (8, 128)) for k in range(3, 5)]
             for q in range(8):
                 rows = pl.ds(8 * q, 8)
-                d = D[u, rows]
-                w = lax.rsqrt(HS[h, rows] + xs[2])
+                d = D[u, rows, pl.ds(0, 128)]
+                w = D[u, rows, pl.ds(128, 128)]
                 r = lax.rsqrt(d)
                 e = lax.erf(d * r * w)
                 m = jnp.maximum(1.0025 - d, 0.0)
@@ -181,7 +182,12 @@
             f = jnp.where(row < 3, v, jnp.where(row < 6, pltpu.roll(v * v, 3, 0), last))
             s1, s2, s3 = split3(f)
             g = jnp.concatenate([s1, s2, s3, s1, s2, s1], axis=0).astype(BF)
-            D[u] = jnp.dot(L[h, :, pl.ds(0, 48)], g, preferred_element_type=F32)
+            oh = jnp.where(types8 == v[5:6], 1.0, 0.0)
+            oh = jnp.concatenate([oh, oh], axis=0).astype(BF)
+            g = jnp.concatenate(
+                [jnp.concatenate([g, zeros16], axis=0), jnp.concatenate([zeros48, oh], axis=0)], axis=1
+            )
+            D[u] = jnp.dot(L[h, :, pl.ds(0, 64)], g, preferred_element_type=F32)
 
     def step(i, carry):
         for k in range(NB):
@@ -197,7 +203,7 @@
             ref[pl.ds(r, 1), :] = jnp.sum(acc[f, pl.ds(2 * r, 2)].reshape(128, 128).T, axis=0, keepdims=True)
         return carry
 
-    lax.fori_loop(0, 32, finish, 0, unroll=4)
+    lax.fori_loop(0, 32, finish, 0, unroll=8)
     s2 = jnp.zeros((32, 128), F32)
     ch = jnp.zeros((32, 128), F32)
     eta = jnp.zeros((32, 128), F32)
@@ -229,12 +235,10 @@
             pltpu.SemaphoreType.DMA((3,)),
             pltpu.VMEM((8 * NR, 128), F32),
             pltpu.VMEM((NT + 1, 8, 128), F32),
-            pltpu.VMEM((64, 64, 128), F32),
             pltpu.VMEM((64, 8, 128), F32),
             pltpu.VMEM((2, 64, 64, 128), F32),
-            pltpu.VMEM((128, 128), F32),
             pltpu.VMEM((64, 64, 128), BF),
-            *[pltpu.VMEM((UN, 64, 128), F32)] * NB,
+            *[pltpu.VMEM((UN, 64, 256), F32)] * NB,
             *[pltpu.VMEM((UN, 8, 128), F32)] * NB,
         ],
         compiler_params=pltpu.CompilerParams(vmem_limit_bytes=60 * 2**20),
@@ -318,7 +322,7 @@
 LINE, SHEET = 16, 32
 
 
-def level_kernel(fe, early, prev, charges, nxt, got, near, far, s1, r1, s2, r2, s3, r3):
+def level_kernel(fe, early, prev, charges, nxt, got, near, far, s1, r1, s2, r2, s3, r3, ready):
     npl = lax.axis_size("plane")
     b, p = lax.axis_index("brick"), lax.axis_index("plane")
     zhi = lax.rem(lax.div(b, 8), 4)
@@ -335,8 +339,8 @@
     sheets = [lax.rem(w + k, SHEET) for k in range(1, SHEET)]
     mates = [lax.rem(p + k, npl) for k in range(1, npl)]
     barrier = pltpu.get_barrier_semaphore()
-    for q in lines:
-        pl.semaphore_signal(barrier, inc=1, device_id=line(q), device_id_type=MESH)
+    for k in (1, 2, 3, 4, 12, 13, 14, 15):
+        pl.semaphore_signal(barrier, inc=1, device_id=line(lax.rem(z + k, LINE)), device_id_type=MESH)
     for q in sheets:
         pl.semaphore_signal(barrier, inc=1, device_id=sheet(q), device_id_type=MESH)
     got[p, 0:72, :] = early[...]
@@ -347,7 +351,9 @@
         return s[0:4] + s[4:8]
 
     near[w] = jnp.concatenate([fold(early[0:32, :] + fe[...]), fold(early[32:64, :])], axis=0)
-    pl.semaphore_wait(barrier, LINE + SHEET - 2)
+    pl.semaphore_wait(barrier, 8 + SHEET - 1)
+    for k in (4, 12):
+        pl.semaphore_signal(ready, inc=1, device_id=line(lax.rem(z + k, LINE)), device_id_type=MESH)
 
     def copy(s, d, ss, rs, to):
         return pltpu.make_async_remote_copy(
@@ -366,6 +372,7 @@
     for k in range(1, SHEET):
         total = total + near[k]
     far[z] = total
+    pl.semaphore_wait(ready, 2)
     second = [copy(far.at[z], far.at[z], s3.at[k], r3.at[k], line(q)) for k, q in enumerate(lines)]
     for c in second:
         c.start()
@@ -417,6 +424,7 @@
             pltpu.VMEM((SHEET, 8, 128), F32),
             pltpu.VMEM((LINE, 8, 128), F32),
             dma((SHEET - 1,)), dma((SHEET - 1,)), dma((3,)), dma((3,)), dma((LINE - 1,)), dma((LINE - 1,)),
+            pltpu.SemaphoreType.REGULAR,
         ],
         compiler_params=pltpu.CompilerParams(collective_id=1, has_side_effects=True),
         name="level",

time: 76.7 us -> 73.3 us (0.956)
  Pallas kernels: 72.9 us -> 69.7 us
    pallas_call x1, Pallas kernels: 14.4 us -> 10.4 us  [pair_call(): pl.pallas_call(pair_kernel, out_shape=[jax.ShapeDtypeStruct((32, 128), F3...]
where the time goes in v4:
time: 73.3 us; the launch traced here: 73 us
  Pallas kernels  69.7 us (95%)
  local copies, waits for them, and re-layouts  1.94 us (3%)
  between operations  1.31 us (2%)
    pallas_call x1, Pallas kernels, finish(): pl.pallas_call(level_kernel, out_shape=[jax.ShapeDtypeStruct((32, 128), F...  39.6 us
    pallas_call x1, Pallas kernels, exchange(): pl.pallas_call(exchange_kernel, out_shape=[jax.ShapeDtypeStruct((7, 32, 1...  19.7 us
    pallas_call x1, Pallas kernels, pair_call(): pl.pallas_call(pair_kernel, out_shape=[jax.ShapeDtypeStruct((32, 128), F3...  10.4 us
    unnamed x4, local copies, waits for them, and re-layouts  1.94 us

profile of v4, /device:TPU:1, one launch (start us, length us, event | category | flops | bytes accessed | tf_op | source)
XLA Modules:
  0.0 73.0 jit_solution(11531481781399959653)
XLA Ops:
  1.3 19.7 %exchange.1 = (f32[7,32,128]{2,1,0:T(8,128)}, f32[4,6,32,128]{3,2,1,0:T(8,128)}, f32[72,128]{1,0:T(8,128)}, s32[1,1792]{1,0:T(1,128)}) custom-call(f32[96,128]{1,0:T(8,128)} %bitcast.11, f32[32,128]{1,0:T(8,128)} %bitcast.12, f32[32,128]{1,0:T(8,128)} %bitcast.13, s32[32,128]{1,0:T(8,128)} %bitcast.14, s32[1,64]{1,0:T(1,128)} %bitcast.20, ...), custom_call_target="tpu_custom_call" | custom-call | tf_op jit(solution)/shard_map/exchange/pallas_call | solution.py:301
  21.0 10.4 %pairs.1 = (f32[32,128]{1,0:T(8,128)}, f32[32,128]{1,0:T(8,128)}) custom-call(s32[1,1792]{1,0:T(1,128)} %get-tuple-element.11.codes_h, f32[8]{0:T(128)} %widths.1, f32[8]{0:T(128)} %chi.1, f32[8]{0:T(128)} %hard.3, f32[7,32,128]{2,1,0:T(8,128)} %get-tuple-element.12.own_h, f32[4,6,32,128]{3,2,1,0:T(8,128)} %get-tuple-element.13.halo_h), custom_call_target="tpu_custom_call" | custom-call | tf_op jit(solution)/shard_map/pairs/pallas_call | solution.py:226
  31.4 39.6 %level.1 = (f32[32,128]{1,0:T(8,128)}, f32[32,128]{1,0:T(8,128)}) custom-call(f32[32,128]{1,0:T(8,128)} %get-tuple-element.14.fe, f32[72,128]{1,0:T(8,128)} %get-tuple-element.15.early, f32[32,128]{1,0:T(8,128)} %bitcast.15), custom_call_target="tpu_custom_call" | custom-call | tf_op jit(solution)/shard_map/level/pallas_call | solution.py:417
  71.0 0.0 copy-start
  71.0 1.3 %copy.18 = f32[1,1,4096]{2,1,0:T(1,128)} copy(f32[1,1,4096]{2,1,0:T(1,128)} %bitcast.17) | data formatting | bytes 32768
  72.4 0.0 copy-done
  72.4 0.6 copy.19
Async XLA Ops:
  71.0 1.3 %copy-start = (f32[32,128]{1,0:T(8,128)S(1)}, f32[32,128]{1,0:T(8,128)}, u32[]{:S(2)}) copy-start(f32[32,128]{1,0:T(8,128)} %get-tuple-element.17) | copy-start | bytes 49156

commit v5 on v4

--- a/solution.py
+++ b/solution.py
@@ -85,44 +85,14 @@
     return a, b, r - b
 
 
-def pair_kernel(codes_h, widths, chi, hard, own_h, halo_h, fe, rf, codes, own, halo, sem, G, C, CH, acc, L, *bufs):
-    loads = [
-        pltpu.make_async_copy(s, d, sem.at[k])
-        for k, (s, d) in enumerate(((own_h, own), (halo_h, halo), (codes_h, codes)))
-    ]
-    for c in loads:
-        c.start()
+def home_features(own, widths, L, CH):
     lane = lax.broadcasted_iota(jnp.int32, (8, 128), 1)
     row = lax.broadcasted_iota(jnp.int32, (8, 128), 0)
     low = lane < 64
-    for c in loads:
-        c.wait()
-    for b in range(5):
-        at = [own[c] if b == 0 else halo[b - 1, c] for c in range(6)]
-        if b in (1, 2):
-            at[0] = at[0] + (-16.0 if b == 1 else 16.0)
-        if b in (3, 4):
-            at[1] = at[1] + (-32.0 if b == 3 else 32.0)
-        for c, x in enumerate((at[0] * 0.1, at[1] * 0.1, at[2] * 0.1, at[3] * 0.1, at[4] * 0.1, at[5])):
-            G[pl.ds(c * NR + b * 32, 32), :] = x
-    G[pl.ds(6 * NR, 2 * NR), :] = jnp.zeros((2 * NR, 128), F32)
-    DS, VS = bufs[:NB], bufs[NB:]
-    for k in range(NB):
-        DS[k][...] = jnp.ones_like(DS[k])
-        VS[k][...] = jnp.zeros_like(VS[k])
 
     def halves(x):
         y = pltpu.roll(x, 64, 1)
         return jnp.where(low, x, y), jnp.where(low, y, x)
-
-    def prep(g, carry):
-        c0, c1 = halves(G[pl.ds(g, 8, stride=NR), :])
-        C[g * 2] = c0
-        C[g * 2 + 1] = c1
-        return carry
-
-    lax.fori_loop(0, NR, prep, 0, unroll=16)
-    C[NT] = jnp.where((row == 3) | (row == 4), 0.0, C[0])
 
     st = jnp.zeros((8, 128), F32)
     for t in range(8):
@@ -130,7 +100,8 @@
     st = st * st * 0.01
 
     def prep_home(r, carry):
-        v = G[pl.ds(r, 8, stride=NR), :]
+        v = own[pl.ds(r, 8, stride=32), :]
+        v = jnp.where(row < 3, v * 0.1, v)
         x = v[:, 0:1]
         y = v[:, 64:65]
         cen = jnp.where(low, jnp.broadcast_to(x, (8, 128)), jnp.broadcast_to(y, (8, 128)))
@@ -147,11 +118,59 @@
         c0, c1 = halves(cen)
         CH[r * 2] = c0
         CH[r * 2 + 1] = c1
-        acc[0, pl.ds(2 * r, 2)] = jnp.zeros((2, 64, 128), F32)
-        acc[1, pl.ds(2 * r, 2)] = jnp.zeros((2, 64, 128), F32)
         return carry
 
     lax.fori_loop(0, 32, prep_home, 0, unroll=8)
+
+
+def pair_kernel(codes_h, widths, chi, hard, own_h, halo_h, feat_h, centre_h, fe, rf, codes, own, halo, L, CH, sem, G, C, acc, *bufs):
+    loads = [
+        pltpu.make_async_copy(s, d, sem.at[k])
+        for k, (s, d) in enumerate(((own_h, own), (halo_h, halo), (codes_h, codes), (feat_h, L), (centre_h, CH)))
+    ]
+    for c in loads:
+        c.start()
+    lane = lax.broadcasted_iota(jnp.int32, (8, 128), 1)
+    row = lax.broadcasted_iota(jnp.int32, (8, 128), 0)
+    low = lane < 64
+    for c in loads[:2]:
+        c.wait()
+    for b in range(5):
+        at = [own[pl.ds(32 * c, 32), :] if b == 0 else halo[b - 1, pl.ds(32 * c, 32), :] for c in range(6)]
+        if b in (1, 2):
+            at[0] = at[0] + (-16.0 if b == 1 else 16.0)
+        if b in (3, 4):
+            at[1] = at[1] + (-32.0 if b == 3 else 32.0)
+        for c, x in enumerate((at[0] * 0.1, at[1] * 0.1, at[2] * 0.1, at[3] * 0.1, at[4] * 0.1, at[5])):
+            G[pl.ds(c * NR + b * 32, 32), :] = x
+    G[pl.ds(6 * NR, 2 * NR), :] = jnp.zeros((2 * NR, 128), F32)
+    DS, VS = bufs[:NB], bufs[NB:]
+    for k in range(NB):
+        DS[k][...] = jnp.ones_like(DS[k])
+        VS[k][...] = jnp.zeros_like(VS[k])
+
+    def halves(x):
+        y = pltpu.roll(x, 64, 1)
+        return jnp.where(low, x, y), jnp.where(low, y, x)
+
+    def prep(g, carry):
+        c0, c1 = halves(G[pl.ds(g, 8, stride=NR), :])
+        C[g * 2] = c0
+        C[g * 2 + 1] = c1
+        return carry
+
+    lax.fori_loop(0, NR, prep, 0, unroll=16)
+
+    def clear(h, carry):
+        acc[0, h] = jnp.zeros((64, 128), F32)
+        acc[1, h] = jnp.zeros((64, 128), F32)
+        return carry
+
+    lax.fori_loop(0, 64, clear, 0, unroll=4)
+    C[NT] = jnp.where((row == 3) | (row == 4), 0.0, C[0])
+
+    for c in loads[2:]:
+        c.wait()
     types8 = row.astype(F32)
     zeros16 = jnp.zeros((16, 128), BF)
     zeros48 = jnp.zeros((48, 128), BF)
@@ -208,46 +227,48 @@
     ch = jnp.zeros((32, 128), F32)
     eta = jnp.zeros((32, 128), F32)
     for t in range(8):
-        hit = own[5] == float(t)
+        hit = own[160:192] == float(t)
         s2 = jnp.where(hit, widths[t] * widths[t], s2)
         ch = jnp.where(hit, chi[t], ch)
         eta = jnp.where(hit, hard[t], eta)
-    itself = own[6] * (2.0 * lax.erf(0.5 * lax.rsqrt(s2 + s2)))
-    residual = rf[...] - itself * own[4]
-    field = ch + (fe[...] - itself * own[3]) + residual
+    itself = own[192:224] * (2.0 * lax.erf(0.5 * lax.rsqrt(s2 + s2)))
+    residual = rf[...] - itself * own[128:160]
+    field = ch + (fe[...] - itself * own[96:128]) + residual
     rf[...] = residual
     fe[...] = field / eta
 
 
-def pair_call(codes, widths, chi, hard, own, halo):
+def pair_call(codes, widths, chi, hard, own, halo, feats, centres):
     sm = pl.BlockSpec(memory_space=pltpu.SMEM)
     vm = pl.BlockSpec(memory_space=pltpu.VMEM)
     hbm = pl.BlockSpec(memory_space=pl.ANY)
     return pl.pallas_call(
         pair_kernel,
         out_shape=[jax.ShapeDtypeStruct((32, 128), F32)] * 2,
-        in_specs=[hbm] + [sm] * 3 + [hbm] * 2,
+        in_specs=[hbm] + [sm] * 3 + [hbm] * 4,
         out_specs=[vm, vm],
         scratch_shapes=[
             pltpu.SMEM(codes.shape, jnp.int32),
             pltpu.VMEM(own.shape, F32),
             pltpu.VMEM(halo.shape, F32),
-            pltpu.SemaphoreType.DMA((3,)),
+            pltpu.VMEM(feats.shape, BF),
+            pltpu.VMEM(centres.shape, F32),
+            pltpu.SemaphoreType.DMA((5,)),
             pltpu.VMEM((8 * NR, 128), F32),
             pltpu.VMEM((NT + 1, 8, 128), F32),
-            pltpu.VMEM((64, 8, 128), F32),
             pltpu.VMEM((2, 64, 64, 128), F32),
-            pltpu.VMEM((64, 64, 128), BF),
             *[pltpu.VMEM((UN, 64, 256), F32)] * NB,
             *[pltpu.VMEM((UN, 8, 128), F32)] * NB,
         ],
         compiler_params=pltpu.CompilerParams(vmem_limit_bytes=60 * 2**20),
         name="pairs",
-    )(codes, widths, chi, hard, own, halo)
+    )(codes, widths, chi, hard, own, halo, feats, centres)
 
 
 def exchange_kernel(
-    pos, aux, resid, types, owner, tiles, cands, hard, count, own, halo, early, codes, send, recv, tr, cr
+    pos_h, aux_h, resid_h, types_h, owner_h, tiles_h, cands_h, hard, widths, count,
+    own_h, halo_h, early_h, codes_h, feat_h, centre_h,
+    pos, aux, resid, types, owner, tiles, cands, own, early, codes, L, CH, tr, cr, load, send, recv, store,
 ):
     nb, npl = lax.axis_size("brick"), lax.axis_size("plane")
     b, p = lax.axis_index("brick"), lax.axis_index("plane")
@@ -256,12 +277,34 @@
     left, right = lax.rem(p + npl - 1, npl), lax.rem(p + 1, npl)
     for d in [(below, p), (above, p), (b, left), (b, right)]:
         pl.semaphore_signal(barrier, inc=1, device_id=d, device_id_type=MESH)
-    for c in range(3):
-        own[c] = pos[pl.ds(32 * c, 32), :]
-    own[3] = aux[...]
-    own[4] = resid[...]
+    ins = ((pos_h, pos), (aux_h, aux), (resid_h, resid), (types_h, types), (owner_h, owner), (tiles_h, tiles), (cands_h, cands))
+    loads = [pltpu.make_async_copy(x, y, load.at[k]) for k, (x, y) in enumerate(ins)]
+    for c in loads:
+        c.start()
+    for c in loads:
+        c.wait()
+    own[0:96, :] = pos[...]
+    own[96:128, :] = aux[...]
+    own[128:160, :] = resid[...]
     ty = types[...].astype(F32)
-    own[5] = ty
+    own[160:192, :] = ty
+    own[192:256, :] = jnp.zeros((64, 128), F32)
+    pl.semaphore_wait(barrier, 4)
+
+    def copy(s, d, k, to):
+        return pltpu.make_async_remote_copy(
+            src_ref=s, dst_ref=d, send_sem=send.at[k], recv_sem=recv.at[k], device_id=to, device_id_type=MESH
+        )
+
+    mine = own.at[pl.ds(0, 192)]
+    copies = [
+        copy(mine, halo_h.at[0], 0, (above, p)),
+        copy(mine, halo_h.at[1], 1, (below, p)),
+        copy(mine, halo_h.at[2], 2, (b, right)),
+        copy(mine, halo_h.at[3], 3, (b, left)),
+    ]
+    for c in copies:
+        c.start()
     inverse = jnp.zeros((32, 128), F32)
     for t in range(8):
         inverse = jnp.where(ty == float(t), 1.0 / jnp.full((32, 128), hard[t], F32), inverse)
@@ -275,54 +318,55 @@
     odds = jnp.dot(ids, jnp.where(inside & (src == 2 * lane + 1), 1.0, 0.0), precision=HI, preferred_element_type=F32)
     r8 = lax.broadcasted_iota(jnp.int32, (8, 128), 0)
     early[64:72, :] = jnp.where(r8 == 0, evens, odds)
-    pl.semaphore_wait(barrier, 4)
-
-    def copy(s, d, k, to):
-        return pltpu.make_async_remote_copy(
-            src_ref=s, dst_ref=d, send_sem=send.at[k], recv_sem=recv.at[k], device_id=to, device_id_type=MESH
-        )
-
-    mine = own.at[pl.ds(0, 6)]
-    copies = [
-        copy(mine, halo.at[0], 0, (above, p)),
-        copy(mine, halo.at[1], 1, (below, p)),
-        copy(mine, halo.at[2], 2, (b, right)),
-        copy(mine, halo.at[3], 3, (b, left)),
-    ]
+    home_features(own, widths, L, CH)
+    own[192:224, :] = order_pairs(tiles, cands, count, codes, tr, cr)
+    outs = ((own, own_h), (early, early_h), (codes, codes_h), (L, feat_h), (CH, centre_h))
+    stores = [pltpu.make_async_copy(x, y, store.at[k]) for k, (x, y) in enumerate(outs)]
+    for c in stores:
+        c.start()
+    for c in stores:
+        c.wait()
     for c in copies:
-        c.start()
-    own[6] = order_pairs(tiles, cands, count, codes, tr, cr)
-    for c in copies:
-        c.wait()
-
-
-def exchange(pos, aux, resid, types, owner, tiles, cands, hard, count):
-    vm = pl.BlockSpec(memory_space=pltpu.VMEM)
+        c.wait()
+
+
+def exchange(pos, aux, resid, types, owner, tiles, cands, hard, widths, count):
+    hbm = pl.BlockSpec(memory_space=pl.ANY)
+    dma = pltpu.SemaphoreType.DMA
+    shape = jax.ShapeDtypeStruct
+    ncodes = (SB + 1) * 128
     return pl.pallas_call(
         exchange_kernel,
         out_shape=[
-            jax.ShapeDtypeStruct((7, 32, 128), F32),
-            jax.ShapeDtypeStruct((4, 6, 32, 128), F32),
-            jax.ShapeDtypeStruct((72, 128), F32),
-            jax.ShapeDtypeStruct((1, (SB + 1) * 128), jnp.int32),
+            shape((256, 128), F32),
+            shape((4, 192, 128), F32),
+            shape((72, 128), F32),
+            shape((1, ncodes), jnp.int32),
+            shape((64, 64, 128), BF),
+            shape((64, 8, 128), F32),
         ],
-        in_specs=[vm] * 7 + [pl.BlockSpec(memory_space=pltpu.SMEM)] * 2,
-        out_specs=[vm] * 4,
-        scratch_shapes=[
-            pltpu.SemaphoreType.DMA((4,)),
-            pltpu.SemaphoreType.DMA((4,)),
+        in_specs=[hbm] * 7 + [pl.BlockSpec(memory_space=pltpu.SMEM)] * 3,
+        out_specs=[hbm] * 6,
+        scratch_shapes=[pltpu.VMEM(x.shape, x.dtype) for x in (pos, aux, resid, types, owner, tiles, cands)]
+        + [
+            pltpu.VMEM((256, 128), F32),
+            pltpu.VMEM((72, 128), F32),
+            pltpu.VMEM((1, ncodes), jnp.int32),
+            pltpu.VMEM((64, 64, 128), BF),
+            pltpu.VMEM((64, 8, 128), F32),
             pltpu.VMEM((128, 128), F32),
             pltpu.VMEM((16, 128), F32),
+            dma((7,)), dma((4,)), dma((4,)), dma((5,)),
         ],
-        compiler_params=pltpu.CompilerParams(collective_id=0, has_side_effects=True),
+        compiler_params=pltpu.CompilerParams(collective_id=0, has_side_effects=True, vmem_limit_bytes=60 * 2**20),
         name="exchange",
-    )(pos, aux, resid, types, owner, tiles, cands, hard, count)
+    )(pos, aux, resid, types, owner, tiles, cands, hard, widths, count)
 
 
 LINE, SHEET = 16, 32
 
 
-def level_kernel(fe, early, prev, charges, nxt, got, near, far, s1, r1, s2, r2, s3, r3, ready):
+def level_kernel(fe_h, early_h, prev_h, charges, nxt, fe, early, prev, load, got, near, far, s1, r1, s2, r2, s3, r3, ready):
     npl = lax.axis_size("plane")
     b, p = lax.axis_index("brick"), lax.axis_index("plane")
     zhi = lax.rem(lax.div(b, 8), 4)
@@ -343,6 +387,12 @@
         pl.semaphore_signal(barrier, inc=1, device_id=line(lax.rem(z + k, LINE)), device_id_type=MESH)
     for q in sheets:
         pl.semaphore_signal(barrier, inc=1, device_id=sheet(q), device_id_type=MESH)
+    ins = ((fe_h, fe), (early_h, early), (prev_h, prev))
+    loads = [pltpu.make_async_copy(x, y, load.at[k]) for k, (x, y) in enumerate(ins)]
+    for c in loads:
+        c.start()
+    for c in loads:
+        c.wait()
     got[p, 0:72, :] = early[...]
     got[p, 72:104, :] = fe[...]
 
@@ -417,22 +467,26 @@
     return pl.pallas_call(
         level_kernel,
         out_shape=[jax.ShapeDtypeStruct((32, 128), F32)] * 2,
-        in_specs=[vm] * 3,
+        in_specs=[pl.BlockSpec(memory_space=pl.ANY)] * 3,
         out_specs=[vm] * 2,
         scratch_shapes=[
+            pltpu.VMEM((32, 128), F32),
+            pltpu.VMEM((72, 128), F32),
+            pltpu.VMEM((32, 128), F32),
+            dma((3,)),
             pltpu.VMEM((4, 104, 128), F32),
             pltpu.VMEM((SHEET, 8, 128), F32),
             pltpu.VMEM((LINE, 8, 128), F32),
             dma((SHEET - 1,)), dma((SHEET - 1,)), dma((3,)), dma((3,)), dma((LINE - 1,)), dma((LINE - 1,)),
             pltpu.SemaphoreType.REGULAR,
         ],
-        compiler_params=pltpu.CompilerParams(collective_id=1, has_side_effects=True),
+        compiler_params=pltpu.CompilerParams(collective_id=1, has_side_effects=True, vmem_limit_bytes=60 * 2**20),
         name="level",
     )(fe, early, prev)
 
 
 def on_device(positions, aux, aux_prev, resid, types, pair_tiles, pair_cands, pair_count, owner_tile, electroneg, hardness, widths):
-    own, halo, early, codes = exchange(
+    own, halo, early, codes, feats, centres = exchange(
         positions.transpose(0, 2, 1, 3).reshape(96, 128),
         aux.reshape(32, 128),
         resid.reshape(32, 128),
@@ -441,9 +495,10 @@
         pair_tiles.reshape(1, -1),
         pair_cands.reshape(1, -1),
         hardness,
+        widths,
         pair_count,
     )
-    fe, rf = pair_call(codes, widths, electroneg, hardness, own, halo)
+    fe, rf = pair_call(codes, widths, electroneg, hardness, own, halo, feats, centres)
     charges, nxt = finish(fe, early, aux_prev.reshape(32, 128))
     return charges.reshape(aux.shape), nxt.reshape(aux.shape), rf.reshape(aux.shape)
 

time: 73.3 us -> 71.3 us (0.973)
  Pallas kernels: 69.7 us -> 67.6 us
    pallas_call x1, Pallas kernels: 10.4 us -> 8.45 us  [pair_call(): pl.pallas_call(pair_kernel, out_shape=[jax.ShapeDtypeStruct((32, 128), F3...]
    pallas_call x1, Pallas kernels: 19.7 us -> 18.9 us  [exchange(): pl.pallas_call(exchange_kernel, out_shape=[shape((256, 128), F32), shape(...]
where the time goes in v5:
time: 71.3 us; the launch traced here: 70.9 us
  Pallas kernels  67.6 us (95%)
  local copies, waits for them, and re-layouts  1.94 us (3%)
  between operations  1.31 us (2%)
    pallas_call x1, Pallas kernels, finish(): pl.pallas_call(level_kernel, out_shape=[jax.ShapeDtypeStruct((32, 128), F...  40.3 us
    pallas_call x1, Pallas kernels, exchange(): pl.pallas_call(exchange_kernel, out_shape=[shape((256, 128), F32), shape(...  18.9 us
    pallas_call x1, Pallas kernels, pair_call(): pl.pallas_call(pair_kernel, out_shape=[jax.ShapeDtypeStruct((32, 128), F3...  8.45 us
    unnamed x4, local copies, waits for them, and re-layouts  1.94 us

profile of v5, /device:TPU:1, one launch (start us, length us, event | category | flops | bytes accessed | tf_op | source)
XLA Modules:
  0.0 70.9 jit_solution(9413835739483606375)
XLA Ops:
  1.3 18.9 %exchange.1 = (f32[256,128]{1,0:T(8,128)}, f32[4,192,128]{2,1,0:T(8,128)}, f32[72,128]{1,0:T(8,128)}, s32[1,1792]{1,0:T(1,128)}, bf16[64,64,128]{2,1,0:T(8,128)(2,1)}, /*index=5*/f32[64,8,128]{2,1,0:T(8,128)}) custom-call(f32[96,128]{1,0:T(8,128)} %bitcast.11, f32[32,128]{1,0:T(8,128)} %bitcast.12, f32[32,128]{1,0:T(8,128)} %bitcast.13, s32[32,128]{1,0:T(8,128)} %bitcast.14, ...), custom_call_target="tpu_custom_call" | custom-call | tf_op jit(solution)/shard_map/exchange/pallas_call | solution.py:338
  20.2 8.5 %pairs.1 = (f32[32,128]{1,0:T(8,128)}, f32[32,128]{1,0:T(8,128)}) custom-call(s32[1,1792]{1,0:T(1,128)} %get-tuple-element.13.codes_h, f32[8]{0:T(128)} %widths.3, f32[8]{0:T(128)} %chi.1, f32[8]{0:T(128)} %hard.3, f32[256,128]{1,0:T(8,128)} %get-tuple-element.14.own_h, f32[4,192,128]{2,1,0:T(8,128)} %get-tuple-element.15.halo_h, ...), custom_call_target="tpu_custom_call" | custom-call | tf_op jit(solution)/shard_map/pairs/pallas_call | solution.py:245
  28.7 40.3 %level.1 = (f32[32,128]{1,0:T(8,128)}, f32[32,128]{1,0:T(8,128)}) custom-call(f32[32,128]{1,0:T(8,128)} %get-tuple-element.18.fe_h, f32[72,128]{1,0:T(8,128)} %get-tuple-element.19.early_h, f32[32,128]{1,0:T(8,128)} %bitcast.15), custom_call_target="tpu_custom_call" | custom-call | tf_op jit(solution)/shard_map/level/pallas_call | solution.py:467
  68.9 0.0 copy-start
  68.9 1.3 %copy.18 = f32[1,1,4096]{2,1,0:T(1,128)} copy(f32[1,1,4096]{2,1,0:T(1,128)} %bitcast.17) | data formatting | bytes 32768
  70.3 0.0 copy-done
  70.3 0.6 copy.19
Async XLA Ops:
  68.9 1.3 %copy-start = (f32[32,128]{1,0:T(8,128)S(1)}, f32[32,128]{1,0:T(8,128)}, u32[]{:S(2)}) copy-start(f32[32,128]{1,0:T(8,128)} %get-tuple-element.21) | copy-start | bytes 49156

commit v6 on v5

--- a/solution.py
+++ b/solution.py
@@ -366,7 +366,7 @@
 LINE, SHEET = 16, 32
 
 
-def level_kernel(fe_h, early_h, prev_h, charges, nxt, fe, early, prev, load, got, near, far, s1, r1, s2, r2, s3, r3, ready):
+def level_kernel(fe_h, early_h, out, fe, early, load, got, near, far, s1, r1, s2, r2, s3, r3, ready):
     npl = lax.axis_size("plane")
     b, p = lax.axis_index("brick"), lax.axis_index("plane")
     zhi = lax.rem(lax.div(b, 8), 4)
@@ -387,7 +387,7 @@
         pl.semaphore_signal(barrier, inc=1, device_id=line(lax.rem(z + k, LINE)), device_id_type=MESH)
     for q in sheets:
         pl.semaphore_signal(barrier, inc=1, device_id=sheet(q), device_id_type=MESH)
-    ins = ((fe_h, fe), (early_h, early), (prev_h, prev))
+    ins = ((fe_h, fe), (early_h, early))
     loads = [pltpu.make_async_copy(x, y, load.at[k]) for k, (x, y) in enumerate(ins)]
     for c in loads:
         c.start()
@@ -397,10 +397,11 @@
     got[p, 72:104, :] = fe[...]
 
     def fold(x):
-        s = x[0:8] + x[8:16] + x[16:24] + x[24:32]
-        return s[0:4] + s[4:8]
-
-    near[w] = jnp.concatenate([fold(early[0:32, :] + fe[...]), fold(early[32:64, :])], axis=0)
+        s = jnp.sum(x, axis=0, keepdims=True)
+        return s + pltpu.roll(s, 64, 1)
+
+    first_half = lax.broadcasted_iota(jnp.int32, (1, 128), 1) < 64
+    near[w] = jnp.where(first_half, fold(early[0:32, :] + fe[...]), fold(early[32:64, :]))
     pl.semaphore_wait(barrier, 8 + SHEET - 1)
     for k in (4, 12):
         pl.semaphore_signal(ready, inc=1, device_id=line(lax.rem(z + k, LINE)), device_id_type=MESH)
@@ -449,40 +450,39 @@
     aux = placed(got[:, 0:32, :].reshape(128, 128))
     inverse = placed(got[:, 32:64, :].reshape(128, 128))
     moved = placed(got[:, 72:104, :].reshape(128, 128))
+    out[0:32, :] = 2.0 * aux - kappa * (moved + aux)
+    out[32:64, :] = kappa * inverse
     for c in second:
         c.wait()
     total = far[0]
     for k in range(1, LINE):
         total = total + far[k]
-    top = jnp.sum(jnp.sum(total[0:4], axis=1, keepdims=True), axis=0, keepdims=True)
-    bottom = jnp.sum(jnp.sum(total[4:8], axis=1, keepdims=True), axis=0, keepdims=True)
-    level = jnp.broadcast_to(top / bottom, (32, 128))
-    charges[...] = level * early[32:64, :] - fe[...]
-    nxt[...] = 2.0 * aux - prev[...] + kappa * (level * inverse - moved - aux)
-
-
-def finish(fe, early, prev):
+    top = jnp.sum(jnp.where(first_half, total, 0.0), axis=1, keepdims=True)
+    bottom = jnp.sum(jnp.where(first_half, 0.0, total), axis=1, keepdims=True)
+    out[64:72, :] = jnp.broadcast_to(top / bottom, (8, 128))
+
+
+def finish(fe, early):
     vm = pl.BlockSpec(memory_space=pltpu.VMEM)
     dma = pltpu.SemaphoreType.DMA
     return pl.pallas_call(
         level_kernel,
-        out_shape=[jax.ShapeDtypeStruct((32, 128), F32)] * 2,
-        in_specs=[pl.BlockSpec(memory_space=pl.ANY)] * 3,
-        out_specs=[vm] * 2,
+        out_shape=jax.ShapeDtypeStruct((72, 128), F32),
+        in_specs=[pl.BlockSpec(memory_space=pl.ANY)] * 2,
+        out_specs=vm,
         scratch_shapes=[
             pltpu.VMEM((32, 128), F32),
             pltpu.VMEM((72, 128), F32),
-            pltpu.VMEM((32, 128), F32),
-            dma((3,)),
+            dma((2,)),
             pltpu.VMEM((4, 104, 128), F32),
-            pltpu.VMEM((SHEET, 8, 128), F32),
-            pltpu.VMEM((LINE, 8, 128), F32),
+            pltpu.VMEM((SHEET, 1, 128), F32),
+            pltpu.VMEM((LINE, 1, 128), F32),
             dma((SHEET - 1,)), dma((SHEET - 1,)), dma((3,)), dma((3,)), dma((LINE - 1,)), dma((LINE - 1,)),
             pltpu.SemaphoreType.REGULAR,
         ],
         compiler_params=pltpu.CompilerParams(collective_id=1, has_side_effects=True, vmem_limit_bytes=60 * 2**20),
         name="level",
-    )(fe, early, prev)
+    )(fe, early)
 
 
 def on_device(positions, aux, aux_prev, resid, types, pair_tiles, pair_cands, pair_count, owner_tile, electroneg, hardness, widths):
@@ -499,7 +499,10 @@
         pair_count,
     )
     fe, rf = pair_call(codes, widths, electroneg, hardness, own, halo, feats, centres)
-    charges, nxt = finish(fe, early, aux_prev.reshape(32, 128))
+    out = finish(fe, early)
+    level = out[64, 0]
+    charges = level * early[32:64] - fe
+    nxt = out[0:32] - aux_prev.reshape(32, 128) + level * out[32:64]
     return charges.reshape(aux.shape), nxt.reshape(aux.shape), rf.reshape(aux.shape)
 
 

time: 71.3 us -> 69.3 us (0.972)
  Pallas kernels: 67.6 us -> 64.4 us
  other arithmetic: 0 us -> 1.93 us
  local copies, waits for them, and re-layouts: 1.94 us -> 1.2 us
    pallas_call x1, Pallas kernels: 40.3 us -> 37.1 us  [finish(): pl.pallas_call(level_kernel, out_shape=jax.ShapeDtypeStruct((72, 128), F3...]
    add x0 -> x1, other arithmetic: none -> 1.93 us  [on_device(): nxt = out[0:32] - aux_prev.reshape(32, 128) + level * out[32:64]]
    unnamed x4, local copies, waits for them, and re-layouts: 1.94 us -> 0.01 us
    slice x0 -> x1, local copies, waits for them, and re-layouts: none -> 1.19 us  [on_device(): level = out[64, 0]]
where the time goes in v6:
time: 69.3 us; the launch traced here: 68.9 us
  Pallas kernels  64.4 us (93%)
  other arithmetic  1.93 us (3%)
  between operations  1.32 us (2%)
  local copies, waits for them, and re-layouts  1.2 us (2%)
    pallas_call x1, Pallas kernels, finish(): pl.pallas_call(level_kernel, out_shape=jax.ShapeDtypeStruct((72, 128), F3...  37.1 us
    pallas_call x1, Pallas kernels, exchange(): pl.pallas_call(exchange_kernel, out_shape=[shape((256, 128), F32), shape(...  18.9 us
    pallas_call x1, Pallas kernels, pair_call(): pl.pallas_call(pair_kernel, out_shape=[jax.ShapeDtypeStruct((32, 128), F3...  8.46 us
    add x1, other arithmetic, on_device(): nxt = out[0:32] - aux_prev.reshape(32, 128) + level * out[32:64]  1.93 us

profile of v6, /device:TPU:1, one launch (start us, length us, event | category | flops | bytes accessed | tf_op | source)
XLA Modules:
  0.0 68.9 jit_solution(10277365428102352267)
XLA Ops:
  1.3 18.9 %exchange.1 = (f32[256,128]{1,0:T(8,128)}, f32[4,192,128]{2,1,0:T(8,128)}, f32[72,128]{1,0:T(8,128)}, s32[1,1792]{1,0:T(1,128)}, bf16[64,64,128]{2,1,0:T(8,128)(2,1)}, /*index=5*/f32[64,8,128]{2,1,0:T(8,128)}) custom-call(f32[96,128]{1,0:T(8,128)} %bitcast.12, f32[32,128]{1,0:T(8,128)} %bitcast.13, f32[32,128]{1,0:T(8,128)} %bitcast.14, s32[32,128]{1,0:T(8,128)} %bitcast.15, ...), custom_call_target="tpu_custom_call" | custom-call | tf_op jit(solution)/shard_map/exchange/pallas_call | solution.py:338
  20.2 8.5 %pairs.1 = (f32[32,128]{1,0:T(8,128)}, f32[32,128]{1,0:T(8,128)}) custom-call(s32[1,1792]{1,0:T(1,128)} %get-tuple-element.11.codes_h, f32[8]{0:T(128)} %widths.3, f32[8]{0:T(128)} %chi.1, f32[8]{0:T(128)} %hard.3, f32[256,128]{1,0:T(8,128)} %get-tuple-element.12.own_h, f32[4,192,128]{2,1,0:T(8,128)} %get-tuple-element.13.halo_h, ...), custom_call_target="tpu_custom_call" | custom-call | tf_op jit(solution)/shard_map/pairs/pallas_call | solution.py:245
  28.7 0.0 copy-start
  28.7 0.0 copy-start.1
  28.7 37.1 %level.1 = f32[72,128]{1,0:T(8,128)} custom-call(f32[32,128]{1,0:T(8,128)} %get-tuple-element.16.fe_h, f32[72,128]{1,0:T(8,128)} %get-tuple-element.17.early_h), custom_call_target="tpu_custom_call" | custom-call | tf_op jit(solution)/shard_map/level/pallas_call | solution.py:468
  65.8 1.2 %slice.12 = f32[1,1]{1,0:T(1,128)} slice(f32[72,128]{1,0:T(8,128)} %level.1), slice={[64:65], [0:1]} | slice | bytes 8 | tf_op jit(solution)/shard_map/slice | solution.py:503
  67.0 0.0 copy-done
  67.0 0.0 copy-done.1
  67.0 1.9 %multiply_add_fusion = (f32[32,128]{1,0:T(8,128)}, f32[32,128]{1,0:T(8,128)}) fusion(f32[72,128]{1,0:T(8,128)} %level.1, f32[32,128]{1,0:T(8,128)S(1)} %bitcast.16, f32[]{:T(128)} %bitcast.7, f32[32,128]{1,0:T(8,128)S(1)} %copy-done, f32[72,128]{1,0:T(8,128)} %get-tuple-element.17.early_h), kind=kLoop, calls=%fused_computation | loop fusion | flops 20480 | bytes 114692 | tf_op jit(solution)/shard_map/add | solution.py:505
Async XLA Ops:
  28.7 38.3 %copy-start = (f32[32,128]{1,0:T(8,128)S(1)}, f32[32,128]{1,0:T(8,128)}, u32[]{:S(2)}) copy-start(f32[32,128]{1,0:T(8,128)} %get-tuple-element.16.fe_h) | copy-start | bytes 49156
  28.7 38.3 %copy-start.1 = (f32[1,1,4096]{2,1,0:T(1,128)S(1)}, f32[1,1,4096]{2,1,0:T(1,128)}, u32[]{:S(2)}) copy-start(f32[1,1,4096]{2,1,0:T(1,128)} %param.14) | copy-start | bytes 49156

commit v7 on v6

--- a/solution.py
+++ b/solution.py
@@ -75,7 +75,7 @@
 
 NR = 160
 UN = 8
-NB = 2
+NB = 4
 
 
 def split3(x):
@@ -133,6 +133,18 @@
     lane = lax.broadcasted_iota(jnp.int32, (8, 128), 1)
     row = lax.broadcasted_iota(jnp.int32, (8, 128), 0)
     low = lane < 64
+    DS, VS = bufs[:NB], bufs[NB:]
+    for k in range(NB):
+        DS[k][...] = jnp.ones_like(DS[k])
+        VS[k][...] = jnp.zeros_like(VS[k])
+
+    def clear(h, carry):
+        acc[0, h] = jnp.zeros((64, 128), F32)
+        acc[1, h] = jnp.zeros((64, 128), F32)
+        return carry
+
+    lax.fori_loop(0, 64, clear, 0, unroll=4)
+
     for c in loads[:2]:
         c.wait()
     for b in range(5):
@@ -144,10 +156,6 @@
         for c, x in enumerate((at[0] * 0.1, at[1] * 0.1, at[2] * 0.1, at[3] * 0.1, at[4] * 0.1, at[5])):
             G[pl.ds(c * NR + b * 32, 32), :] = x
     G[pl.ds(6 * NR, 2 * NR), :] = jnp.zeros((2 * NR, 128), F32)
-    DS, VS = bufs[:NB], bufs[NB:]
-    for k in range(NB):
-        DS[k][...] = jnp.ones_like(DS[k])
-        VS[k][...] = jnp.zeros_like(VS[k])
 
     def halves(x):
         y = pltpu.roll(x, 64, 1)
@@ -161,12 +169,6 @@
 
     lax.fori_loop(0, NR, prep, 0, unroll=16)
 
-    def clear(h, carry):
-        acc[0, h] = jnp.zeros((64, 128), F32)
-        acc[1, h] = jnp.zeros((64, 128), F32)
-        return carry
-
-    lax.fori_loop(0, 64, clear, 0, unroll=4)
     C[NT] = jnp.where((row == 3) | (row == 4), 0.0, C[0])
 
     for c in loads[2:]:
@@ -485,6 +487,23 @@
     )(fe, early)
 
 
+def last_kernel(out, fe, early, prev, charges, nxt):
+    level = jnp.broadcast_to(out[64:65, :], (32, 128))
+    charges[...] = level * early[32:64, :] - fe[...]
+    nxt[...] = out[0:32, :] - prev[...] + level * out[32:64, :]
+
+
+def last_step(out, fe, early, prev):
+    vm = pl.BlockSpec(memory_space=pltpu.VMEM)
+    return pl.pallas_call(
+        last_kernel,
+        out_shape=[jax.ShapeDtypeStruct((32, 128), F32)] * 2,
+        in_specs=[vm] * 4,
+        out_specs=[vm] * 2,
+        name="last_step",
+    )(out, fe, early, prev)
+
+
 def on_device(positions, aux, aux_prev, resid, types, pair_tiles, pair_cands, pair_count, owner_tile, electroneg, hardness, widths):
     own, halo, early, codes, feats, centres = exchange(
         positions.transpose(0, 2, 1, 3).reshape(96, 128),
@@ -500,9 +519,7 @@
     )
     fe, rf = pair_call(codes, widths, electroneg, hardness, own, halo, feats, centres)
     out = finish(fe, early)
-    level = out[64, 0]
-    charges = level * early[32:64] - fe
-    nxt = out[0:32] - aux_prev.reshape(32, 128) + level * out[32:64]
+    charges, nxt = last_step(out, fe, early, aux_prev.reshape(32, 128))
     return charges.reshape(aux.shape), nxt.reshape(aux.shape), rf.reshape(aux.shape)
 
 

time: 69.3 us -> 68.2 us (0.984)
  Pallas kernels: 64.4 us -> 66.5 us
  other arithmetic: 1.93 us -> 0 us
  local copies, waits for them, and re-layouts: 1.2 us -> 0 us
    add x1 -> x0, other arithmetic: 1.93 us -> none  [on_device(): nxt = out[0:32] - aux_prev.reshape(32, 128) + level * out[32:64]]
    pallas_call x1, Pallas kernels: 8.46 us -> 10.2 us  [pair_call(): pl.pallas_call(pair_kernel, out_shape=[jax.ShapeDtypeStruct((32, 128), F3...]
    pallas_call x0 -> x1, Pallas kernels: none -> 1.42 us  [last_step(): pl.pallas_call(last_kernel, out_shape=[jax.ShapeDtypeStruct((32, 128), F3...]
    slice x1 -> x0, local copies, waits for them, and re-layouts: 1.19 us -> none  [on_device(): level = out[64, 0]]
    pallas_call x1, Pallas kernels: 37.1 us -> 36 us  [finish(): pl.pallas_call(level_kernel, out_shape=jax.ShapeDtypeStruct((72, 128), F3...]
where the time goes in v7:
time: 68.2 us; the launch traced here: 67.8 us
  Pallas kernels  66.5 us (98%)
  between operations  1.3 us (2%)
    pallas_call x1, Pallas kernels, finish(): pl.pallas_call(level_kernel, out_shape=jax.ShapeDtypeStruct((72, 128), F3...  36 us
    pallas_call x1, Pallas kernels, exchange(): pl.pallas_call(exchange_kernel, out_shape=[shape((256, 128), F32), shape(...  18.9 us
    pallas_call x1, Pallas kernels, pair_call(): pl.pallas_call(pair_kernel, out_shape=[jax.ShapeDtypeStruct((32, 128), F3...  10.2 us
    pallas_call x1, Pallas kernels, last_step(): pl.pallas_call(last_kernel, out_shape=[jax.ShapeDtypeStruct((32, 128), F3...  1.42 us

profile of v7, /device:TPU:1, one launch (start us, length us, event | category | flops | bytes accessed | tf_op | source)
XLA Modules:
  0.0 67.8 jit_solution(4417181990204862545)
XLA Ops:
  1.3 18.9 %exchange.1 = (f32[256,128]{1,0:T(8,128)}, f32[4,192,128]{2,1,0:T(8,128)}, f32[72,128]{1,0:T(8,128)}, s32[1,1792]{1,0:T(1,128)}, bf16[64,64,128]{2,1,0:T(8,128)(2,1)}, /*index=5*/f32[64,8,128]{2,1,0:T(8,128)}) custom-call(f32[96,128]{1,0:T(8,128)} %bitcast.11, f32[32,128]{1,0:T(8,128)} %bitcast.12, f32[32,128]{1,0:T(8,128)} %bitcast.13, s32[32,128]{1,0:T(8,128)} %bitcast.14, ...), custom_call_target="tpu_custom_call" | custom-call | tf_op jit(solution)/shard_map/exchange/pallas_call | solution.py:340
  20.2 10.2 %pairs.1 = (f32[32,128]{1,0:T(8,128)}, f32[32,128]{1,0:T(8,128)}) custom-call(s32[1,1792]{1,0:T(1,128)} %get-tuple-element.13.codes_h, f32[8]{0:T(128)} %widths.3, f32[8]{0:T(128)} %chi.1, f32[8]{0:T(128)} %hard.3, f32[256,128]{1,0:T(8,128)} %get-tuple-element.14.own_h, f32[4,192,128]{2,1,0:T(8,128)} %get-tuple-element.15.halo_h, ...), custom_call_target="tpu_custom_call" | custom-call | tf_op jit(solution)/shard_map/pairs/pallas_call | solution.py:247
  30.4 36.0 %level.1.out = f32[72,128]{1,0:T(8,128)} custom-call(f32[32,128]{1,0:T(8,128)} %get-tuple-element.18.fe_h.fe, f32[72,128]{1,0:T(8,128)} %get-tuple-element.19.early_h.early), custom_call_target="tpu_custom_call" | custom-call | tf_op jit(solution)/shard_map/level/pallas_call | solution.py:470
  66.4 1.4 %last_step.1 = (f32[32,128]{1,0:T(8,128)}, f32[32,128]{1,0:T(8,128)}) custom-call(f32[72,128]{1,0:T(8,128)} %level.1.out, f32[32,128]{1,0:T(8,128)} %get-tuple-element.18.fe_h.fe, f32[72,128]{1,0:T(8,128)} %get-tuple-element.19.early_h.early, f32[32,128]{1,0:T(8,128)} %bitcast.15), custom_call_target="tpu_custom_call" | custom-call | tf_op jit(solution)/shard_map/last_step/pallas_call | solution.py:498

commit v8 on v7

--- a/solution.py
+++ b/solution.py
@@ -75,7 +75,7 @@
 
 NR = 160
 UN = 8
-NB = 4
+NB = 2
 
 
 def split3(x):

time: 68.2 us -> 67.1 us (0.984)
  Pallas kernels: 66.5 us -> 65.4 us
    pallas_call x1, Pallas kernels: 36 us -> 34.5 us  [finish(): pl.pallas_call(level_kernel, out_shape=jax.ShapeDtypeStruct((72, 128), F3...]
where the time goes in v8:
time: 67.1 us; the launch traced here: 66.7 us
  Pallas kernels  65.4 us (97%)
  between operations  1.3 us (2%)
    pallas_call x1, Pallas kernels, finish(): pl.pallas_call(level_kernel, out_shape=jax.ShapeDtypeStruct((72, 128), F3...  34.5 us
    pallas_call x1, Pallas kernels, exchange(): pl.pallas_call(exchange_kernel, out_shape=[shape((256, 128), F32), shape(...  18.9 us
    pallas_call x1, Pallas kernels, pair_call(): pl.pallas_call(pair_kernel, out_shape=[jax.ShapeDtypeStruct((32, 128), F3...  10.6 us
    pallas_call x1, Pallas kernels, last_step(): pl.pallas_call(last_kernel, out_shape=[jax.ShapeDtypeStruct((32, 128), F3...  1.42 us

profile of v8, /device:TPU:1, one launch (start us, length us, event | category | flops | bytes accessed | tf_op | source)
XLA Modules:
  0.0 66.7 jit_solution(12705722156728297421)
XLA Ops:
  1.3 18.9 %exchange.1 = (f32[256,128]{1,0:T(8,128)}, f32[4,192,128]{2,1,0:T(8,128)}, f32[72,128]{1,0:T(8,128)}, s32[1,1792]{1,0:T(1,128)}, bf16[64,64,128]{2,1,0:T(8,128)(2,1)}, /*index=5*/f32[64,8,128]{2,1,0:T(8,128)}) custom-call(f32[96,128]{1,0:T(8,128)} %bitcast.11, f32[32,128]{1,0:T(8,128)} %bitcast.12, f32[32,128]{1,0:T(8,128)} %bitcast.13, s32[32,128]{1,0:T(8,128)} %bitcast.14, ...), custom_call_target="tpu_custom_call" | custom-call | tf_op jit(solution)/shard_map/exchange/pallas_call | solution.py:340
  20.2 10.6 %pairs.1 = (f32[32,128]{1,0:T(8,128)}, f32[32,128]{1,0:T(8,128)}) custom-call(s32[1,1792]{1,0:T(1,128)} %get-tuple-element.13.codes_h, f32[8]{0:T(128)} %widths.3, f32[8]{0:T(128)} %chi.1, f32[8]{0:T(128)} %hard.3, f32[256,128]{1,0:T(8,128)} %get-tuple-element.14.own_h, f32[4,192,128]{2,1,0:T(8,128)} %get-tuple-element.15.halo_h, ...), custom_call_target="tpu_custom_call" | custom-call | tf_op jit(solution)/shard_map/pairs/pallas_call | solution.py:247
  30.8 34.5 %level.1.out = f32[72,128]{1,0:T(8,128)} custom-call(f32[32,128]{1,0:T(8,128)} %get-tuple-element.18.fe_h.fe, f32[72,128]{1,0:T(8,128)} %get-tuple-element.19.early_h.early), custom_call_target="tpu_custom_call" | custom-call | tf_op jit(solution)/shard_map/level/pallas_call | solution.py:470
  65.3 1.4 %last_step.1 = (f32[32,128]{1,0:T(8,128)}, f32[32,128]{1,0:T(8,128)}) custom-call(f32[72,128]{1,0:T(8,128)} %level.1.out, f32[32,128]{1,0:T(8,128)} %get-tuple-element.18.fe_h.fe, f32[72,128]{1,0:T(8,128)} %get-tuple-element.19.early_h.early, f32[32,128]{1,0:T(8,128)} %bitcast.15), custom_call_target="tpu_custom_call" | custom-call | tf_op jit(solution)/shard_map/last_step/pallas_call | solution.py:498

commit v9 on v8

--- a/solution.py
+++ b/solution.py
@@ -381,11 +381,11 @@
     def sheet(q):
         return (32 * lax.div(q, 8) + 8 * zhi + lax.rem(q, 8), p)
 
-    lines = [lax.rem(z + k, LINE) for k in range(1, LINE)]
-    sheets = [lax.rem(w + k, SHEET) for k in range(1, SHEET)]
+    lines = [lax.rem(z + k, LINE) for k in sorted(range(1, LINE), key=lambda k: abs(2 * k - LINE))]
+    sheets = [lax.rem(w + k, SHEET) for k in sorted(range(1, SHEET), key=lambda k: abs(2 * k - SHEET))]
     mates = [lax.rem(p + k, npl) for k in range(1, npl)]
     barrier = pltpu.get_barrier_semaphore()
-    for k in (1, 2, 3, 4, 12, 13, 14, 15):
+    for k in (4, 12, 3, 13, 2, 14, 1, 15):
         pl.semaphore_signal(barrier, inc=1, device_id=line(lax.rem(z + k, LINE)), device_id_type=MESH)
     for q in sheets:
         pl.semaphore_signal(barrier, inc=1, device_id=sheet(q), device_id_type=MESH)

time: 67.1 us -> 67 us (level)
    pallas_call x1, Pallas kernels: 10.6 us -> 9.86 us  [pair_call(): pl.pallas_call(pair_kernel, out_shape=[jax.ShapeDtypeStruct((32, 128), F3...]
where the time goes in v9:
time: 67 us; the launch traced here: 66.6 us
  Pallas kernels  65.3 us (97%)
  between operations  1.3 us (2%)
    pallas_call x1, Pallas kernels, finish(): pl.pallas_call(level_kernel, out_shape=jax.ShapeDtypeStruct((72, 128), F3...  35.1 us
    pallas_call x1, Pallas kernels, exchange(): pl.pallas_call(exchange_kernel, out_shape=[shape((256, 128), F32), shape(...  18.9 us
    pallas_call x1, Pallas kernels, pair_call(): pl.pallas_call(pair_kernel, out_shape=[jax.ShapeDtypeStruct((32, 128), F3...  9.86 us
    pallas_call x1, Pallas kernels, last_step(): pl.pallas_call(last_kernel, out_shape=[jax.ShapeDtypeStruct((32, 128), F3...  1.42 us

profile of v9, /device:TPU:1, one launch (start us, length us, event | category | flops | bytes accessed | tf_op | source)
XLA Modules:
  0.0 66.6 jit_solution(14453842039490597693)
XLA Ops:
  1.3 18.9 %exchange.1 = (f32[256,128]{1,0:T(8,128)}, f32[4,192,128]{2,1,0:T(8,128)}, f32[72,128]{1,0:T(8,128)}, s32[1,1792]{1,0:T(1,128)}, bf16[64,64,128]{2,1,0:T(8,128)(2,1)}, /*index=5*/f32[64,8,128]{2,1,0:T(8,128)}) custom-call(f32[96,128]{1,0:T(8,128)} %bitcast.11, f32[32,128]{1,0:T(8,128)} %bitcast.12, f32[32,128]{1,0:T(8,128)} %bitcast.13, s32[32,128]{1,0:T(8,128)} %bitcast.14, ...), custom_call_target="tpu_custom_call" | custom-call | tf_op jit(solution)/shard_map/exchange/pallas_call | solution.py:340
  20.2 9.9 %pairs.1 = (f32[32,128]{1,0:T(8,128)}, f32[32,128]{1,0:T(8,128)}) custom-call(s32[1,1792]{1,0:T(1,128)} %get-tuple-element.13.codes_h, f32[8]{0:T(128)} %widths.3, f32[8]{0:T(128)} %chi.1, f32[8]{0:T(128)} %hard.3, f32[256,128]{1,0:T(8,128)} %get-tuple-element.14.own_h, f32[4,192,128]{2,1,0:T(8,128)} %get-tuple-element.15.halo_h, ...), custom_call_target="tpu_custom_call" | custom-call | tf_op jit(solution)/shard_map/pairs/pallas_call | solution.py:247
  30.1 35.1 %level.1.out = f32[72,128]{1,0:T(8,128)} custom-call(f32[32,128]{1,0:T(8,128)} %get-tuple-element.18.fe_h.fe, f32[72,128]{1,0:T(8,128)} %get-tuple-element.19.early_h.early), custom_call_target="tpu_custom_call" | custom-call | tf_op jit(solution)/shard_map/level/pallas_call | solution.py:470
  65.2 1.4 %last_step.1 = (f32[32,128]{1,0:T(8,128)}, f32[32,128]{1,0:T(8,128)}) custom-call(f32[72,128]{1,0:T(8,128)} %level.1.out, f32[32,128]{1,0:T(8,128)} %get-tuple-element.18.fe_h.fe, f32[72,128]{1,0:T(8,128)} %get-tuple-element.19.early_h.early, f32[32,128]{1,0:T(8,128)} %bitcast.15), custom_call_target="tpu_custom_call" | custom-call | tf_op jit(solution)/shard_map/last_step/pallas_call | solution.py:498

commit v10 on v9

--- a/solution.py
+++ b/solution.py
@@ -224,7 +224,7 @@
             ref[pl.ds(r, 1), :] = jnp.sum(acc[f, pl.ds(2 * r, 2)].reshape(128, 128).T, axis=0, keepdims=True)
         return carry
 
-    lax.fori_loop(0, 32, finish, 0, unroll=8)
+    lax.fori_loop(0, 32, finish, 0, unroll=16)
     s2 = jnp.zeros((32, 128), F32)
     ch = jnp.zeros((32, 128), F32)
     eta = jnp.zeros((32, 128), F32)

time: 67 us -> 66.9 us (level)
    pallas_call x1, Pallas kernels: 9.86 us -> 9.01 us  [pair_call(): pl.pallas_call(pair_kernel, out_shape=[jax.ShapeDtypeStruct((32, 128), F3...]
    pallas_call x1, Pallas kernels: 35.1 us -> 35.8 us  [finish(): pl.pallas_call(level_kernel, out_shape=jax.ShapeDtypeStruct((72, 128), F3...]
where the time goes in v10:
time: 66.9 us; the launch traced here: 66.5 us
  Pallas kernels  65.2 us (97%)
  between operations  1.3 us (2%)
    pallas_call x1, Pallas kernels, finish(): pl.pallas_call(level_kernel, out_shape=jax.ShapeDtypeStruct((72, 128), F3...  35.8 us
    pallas_call x1, Pallas kernels, exchange(): pl.pallas_call(exchange_kernel, out_shape=[shape((256, 128), F32), shape(...  18.9 us
    pallas_call x1, Pallas kernels, pair_call(): pl.pallas_call(pair_kernel, out_shape=[jax.ShapeDtypeStruct((32, 128), F3...  9.01 us
    pallas_call x1, Pallas kernels, last_step(): pl.pallas_call(last_kernel, out_shape=[jax.ShapeDtypeStruct((32, 128), F3...  1.42 us

profile of v10, /device:TPU:1, one launch (start us, length us, event | category | flops | bytes accessed | tf_op | source)
XLA Modules:
  0.0 66.5 jit_solution(11940617101937902933)
XLA Ops:
  1.3 18.9 %exchange.1 = (f32[256,128]{1,0:T(8,128)}, f32[4,192,128]{2,1,0:T(8,128)}, f32[72,128]{1,0:T(8,128)}, s32[1,1792]{1,0:T(1,128)}, bf16[64,64,128]{2,1,0:T(8,128)(2,1)}, /*index=5*/f32[64,8,128]{2,1,0:T(8,128)}) custom-call(f32[96,128]{1,0:T(8,128)} %bitcast.11, f32[32,128]{1,0:T(8,128)} %bitcast.12, f32[32,128]{1,0:T(8,128)} %bitcast.13, s32[32,128]{1,0:T(8,128)} %bitcast.14, ...), custom_call_target="tpu_custom_call" | custom-call | tf_op jit(solution)/shard_map/exchange/pallas_call | solution.py:340
  20.2 9.0 %pairs.1 = (f32[32,128]{1,0:T(8,128)}, f32[32,128]{1,0:T(8,128)}) custom-call(s32[1,1792]{1,0:T(1,128)} %get-tuple-element.13.codes_h, f32[8]{0:T(128)} %widths.3, f32[8]{0:T(128)} %chi.1, f32[8]{0:T(128)} %hard.3, f32[256,128]{1,0:T(8,128)} %get-tuple-element.14.own_h, f32[4,192,128]{2,1,0:T(8,128)} %get-tuple-element.15.halo_h, ...), custom_call_target="tpu_custom_call" | custom-call | tf_op jit(solution)/shard_map/pairs/pallas_call | solution.py:247
  29.2 35.8 %level.1.out = f32[72,128]{1,0:T(8,128)} custom-call(f32[32,128]{1,0:T(8,128)} %get-tuple-element.18.fe_h.fe, f32[72,128]{1,0:T(8,128)} %get-tuple-element.19.early_h.early), custom_call_target="tpu_custom_call" | custom-call | tf_op jit(solution)/shard_map/level/pallas_call | solution.py:470
  65.1 1.4 %last_step.1 = (f32[32,128]{1,0:T(8,128)}, f32[32,128]{1,0:T(8,128)}) custom-call(f32[72,128]{1,0:T(8,128)} %level.1.out, f32[32,128]{1,0:T(8,128)} %get-tuple-element.18.fe_h.fe, f32[72,128]{1,0:T(8,128)} %get-tuple-element.19.early_h.early, f32[32,128]{1,0:T(8,128)} %bitcast.15), custom_call_target="tpu_custom_call" | custom-call | tf_op jit(solution)/shard_map/last_step/pallas_call | solution.py:498
